TPU v7x, 128 devices: a whole 4x4x4 slice. The times are simulated.
128 devices in a mesh: path: 16 (over z, y), mp: 8 (over x, core).
Axes of the slice: x: 4, y: 4, z: 4, core: 2. Of those that a mesh axis runs over, the one named last changes fastest.
Arguments:
- features: bfloat16 [8192, 4096], P(('path', 'mp')), may hold values from -6 to 6
- targets: bfloat16 [8192, 4096], P('path', 'mp'), may hold values from -3 to 3
- module_table: bfloat16 [16, 4096, 4096], P(None, ('path', 'mp')), may hold values from -0.09375 to 0.09375
- momentum: bfloat16 [16, 4096, 4096], P(None, ('path', 'mp')), may hold values from -0.049804688 to 0.049804688
- path_lists: int32 [16, 2], replicated, may hold values from 0 to 15, all different within a row
Outputs:
- momentum_out: bfloat16 [16, 4096, 4096], P(None, ('path', 'mp'))
- evaluated: bfloat16 [8192, 4096], P('path', 'mp')
Inputs may be any that keep to these rules, and one draw needn't show every extreme that they name: `path_lists`: each path names 2 different modules, and every module is named by at least one path.
All inputs are finite; a program needn't handle non-finite values.
Results may differ from a plain program's by a relative error of at most 0.0075.
The roundings to bfloat16 on the way count: a program that leaves them out, or rounds other values in their place, can miss the bound.
Values may be sent and summed in bfloat16 or wider, within the bound.
A program may use at most 128 MiB of HBM per device.

v0:
```python
import jax
import jax.numpy as jnp
from jax import lax
from jax.sharding import PartitionSpec as P

INNER = 2
TOK_PATH = 512


beta_first = 0.9
beta_second = 0.95
adam_epsilon = 1e-05
inner_rate = 0.004
weight_decay = 0.1
outer_rate = 0.7
outer_momentum = 0.9


def normalize(features):
    values = features.astype(jnp.float32)
    factor = lax.rsqrt(jnp.mean(values * values, axis=-1, keepdims=True) + 1e-05)
    return (values * factor).astype(jnp.bfloat16)


def adam_update(master, first, second, gradient, counter):
    first = beta_first * first + (1.0 - beta_first) * gradient
    second = beta_second * second + (1.0 - beta_second) * gradient * gradient
    first_hat = first / (1.0 - beta_first**counter)
    second_hat = second / (1.0 - beta_second**counter)
    master = master - inner_rate * (
        first_hat / (jnp.sqrt(second_hat) + adam_epsilon) + weight_decay * master
    )
    return (master, first, second)


def path_round(normed, target, start):
    master = start.astype(jnp.float32)
    first = jnp.zeros_like(master)
    second = jnp.zeros_like(master)
    current = start
    wide = normed.astype(jnp.float32)
    goal = target.astype(jnp.float32)
    for iteration in range(1, INNER + 1):
        both = jnp.einsum("td,kdc->ktc", normed, current, preferred_element_type=jnp.float32)
        gate_act = both[0]
        up_act = both[1]
        sigma = jax.nn.sigmoid(gate_act)
        swish = gate_act * sigma
        error = (swish * up_act - goal) / TOK_PATH
        d_gate = error * up_act * sigma * (1.0 + gate_act * (1.0 - sigma))
        d_up = error * swish
        slopes = jnp.stack([d_gate, d_up])
        gradient = jnp.einsum(
            "td,ktc->kdc",
            wide,
            slopes,
            precision=lax.Precision.HIGHEST,
            preferred_element_type=jnp.float32,
        )
        master, first, second = adam_update(master, first, second, gradient, iteration)
        current = master.astype(jnp.bfloat16)
    return (start.astype(jnp.float32) - master).astype(jnp.bfloat16)


def move_blocks(buffer, paths, shards):
    flattened = buffer.reshape((paths * shards,) + buffer.shape[2:])
    arrived = lax.all_to_all(flattened, ("path", "mp"), split_axis=0, concat_axis=0, tiled=True)
    return arrived.reshape(buffer.shape)


def local(features, targets, module_table, momentum, path_lists):
    paths = lax.axis_size("path")
    shards = lax.axis_size("mp")
    modules, rows_own, width = module_table.shape
    columns = width // shards
    slots = path_lists.shape[1]
    flat_lists = path_lists.reshape(-1)
    normed = lax.all_gather(normalize(features), "mp", axis=0, tiled=True)

    def deliver(table):
        picked = jnp.take(table, flat_lists, axis=0).reshape(
            paths, slots, rows_own, shards, columns
        )
        outgoing = jnp.transpose(picked, (0, 3, 1, 2, 4))
        arrived = move_blocks(outgoing, paths, shards)
        return jnp.transpose(arrived, (2, 0, 1, 3, 4)).reshape(slots, width, columns)

    start = deliver(module_table)
    delta = path_round(normed, targets, start)
    outgoing = jnp.transpose(
        delta.reshape(slots, paths, shards, rows_own, columns), (1, 2, 0, 3, 4)
    )
    arrived = move_blocks(outgoing, paths, shards)
    row_blocks = jnp.transpose(arrived, (0, 2, 3, 1, 4)).reshape(paths * slots, rows_own, width)
    select = flat_lists[None, :] == jnp.arange(modules, dtype=jnp.int32)[:, None]
    counts = jnp.sum(select.astype(jnp.float32), axis=1)
    sums = jnp.einsum(
        "ms,srw->mrw", select.astype(jnp.bfloat16), row_blocks, preferred_element_type=jnp.float32
    )
    average = sums / counts[:, None, None]
    moment = outer_momentum * momentum.astype(jnp.float32) + average
    updated = (
        module_table.astype(jnp.float32) - outer_rate * (average + outer_momentum * moment)
    ).astype(jnp.bfloat16)
    fresh = deliver(updated)
    both = jnp.einsum("td,kdc->ktc", normed, fresh, preferred_element_type=jnp.float32)
    evaluated = (jax.nn.silu(both[0]) * both[1]).astype(jnp.bfloat16)
    return (moment.astype(jnp.bfloat16), evaluated)


def solution(mesh):
    return jax.shard_map(
        local,
        mesh=mesh,
        in_specs=(
            P(("path", "mp"), None),
            P("path", "mp"),
            P(None, ("path", "mp"), None),
            P(None, ("path", "mp"), None),
            P(),
        ),
        out_specs=(P(None, ("path", "mp"), None), P("path", "mp")),
        check_vma=False,
    )
```

profile of v0, /device:TPU:1, one launch (start us, length us, event | category | flops | bytes accessed | tf_op | source)
XLA Modules:
  0.0 618.3 jit_solution(8661559169963559141)
XLA Ops:
  7.2 0.8 copy.30
  7.9 0.1 eq.15
  8.0 0.0 copy-start.5
  8.0 0.0 copy-start.3
  8.1 0.0 copy-start.2
  8.1 7.2 %gather_fusion = bf16[32,32,4096]{2,1,0:T(8,128)(2,1)} fusion(bf16[16,32,4096]{2,1,0:T(8,128)(2,1)} %param.9, s32[1024]{0:T(1024)S(1)} %pad_clamp_fusion), kind=kCustom, calls=%fused_computation.clone | custom fusion | bytes 16777344 | tf_op jit(solution)/shard_map/jit(_take)/gather | solution.py:81
  15.3 0.0 copy-done.3
  15.3 7.5 %broadcast_select_fusion.1 = bf16[32,32,4096]{2,1,0:T(8,128)(2,1)} fusion(bf16[32,32,4096]{2,1,0:T(8,128)(2,1)} %gather_fusion, pred[32]{0:T(512)(128)(4,1)S(1)} %compare_and_fusion), kind=kLoop, calls=%fused_computation.27 | loop fusion | flops 4194304 | bytes 16777248 | tf_op jit(solution)/shard_map/jit(_take)/select_n | solution.py:81
  22.8 12.2 %copy.48 = bf16[128,8,8,512]{3,2,1,0:T(8,128)(2,1)} copy(bf16[128,8,8,512]{3,1,2,0:T(8,128)(2,1)} %bitcast.150) | data formatting | bytes 16777216
  35.0 10.2 %copy.31 = bf16[16,8,2,32,512]{4,3,2,1,0:T(8,128)(2,1)} copy(bf16[16,8,2,32,512]{4,1,3,2,0:T(8,128)(2,1)} %bitcast.155) | data formatting | bytes 16777216 | tf_op jit(solution)/shard_map/transpose | solution.py:84
  45.1 12.0 %all-to-all-start = ((bf16[128,2,32,512]{3,2,1,0:T(8,128)(2,1)}), bf16[128,2,32,512]{3,2,1,0:T(8,128)(2,1)}, u32[]{:S(2)}, u32[]{:S(2)}) async-start(bf16[128,2,32,512]{3,2,1,0:T(8,128)(2,1)} %bitcast.151), calls=%async_computation | async-start | bytes 16777216 | tf_op jit(solution)/shard_map/all_to_all | solution.py:67
  57.1 0.0 all-gather.2.cloned.1.call-start
  57.2 0.0 copy-done
  57.2 0.2 fusion.42
  57.4 1.0 fusion.43
  58.3 0.0 all-gather.2.cloned.1.call-update
  58.4 0.2 copy.35
  58.6 113.2 %all-to-all-done = bf16[128,2,32,512]{3,2,1,0:T(8,128)(2,1)} async-done(((bf16[128,2,32,512]{3,2,1,0:T(8,128)(2,1)}), bf16[128,2,32,512]{3,2,1,0:T(8,128)(2,1)}, u32[]{:S(2)}, u32[]{:S(2)}) %all-to-all-start) | async-done | bytes 8388640 | tf_op jit(solution)/shard_map/all_to_all | solution.py:67
  171.8 8.3 %copy.32 = bf16[16,8,2,32,512]{4,3,1,0,2:T(8,128)(2,1)} copy(bf16[16,8,2,32,512]{4,3,2,1,0:T(8,128)(2,1)} %bitcast.3) | data formatting | bytes 16777216 | tf_op jit(solution)/shard_map/reshape | solution.py:68
  180.1 11.3 %copy.33 = bf16[2,4096,512]{1,2,0:T(8,128)(2,1)} copy(bf16[2,4096,512]{2,1,0:T(8,128)(2,1)} %bitcast.153) | data formatting | bytes 16777216 | tf_op jit(solution)/shard_map/reshape | solution.py:86
  191.4 8.4 %fusion.31 = f32[2,512,512]{1,2,0:T(8,128)S(1)} fusion(bf16[2,4096,512]{2,1,0:T(8,128)(2,1)} %bitcast.154, bf16[512,4096]{1,0:T(8,128)(2,1)} %all-gather.2.cloned.1.call-done), kind=kOutput, calls=%fused_computation.44 | convolution fusion | flops 4294967296 | bytes 14680064 | tf_op jit(solution)/shard_map/td,kdc->ktc/dot_general | solution.py:44
  199.8 0.0 slice-start
  199.8 0.6 multiply_bitcast_fusion.3
  200.4 0.0 slice-start.1
  200.4 15.8 %fusion.19 = f32[2,512,4096]{2,1,0:T(8,128)} fusion(bf16[512,4096]{1,0:T(8,128)(2,1)S(1)} %copy-done.7, f32[1,512,512]{1,2,0:T(8,128)S(1)} %get-tuple-element.14, f32[1,512,512]{1,2,0:T(8,128)S(1)} %get-tuple-element.13), kind=kOutput, calls=%fused_computation.34 | convolution fusion | flops 25770328064 | bytes 23068672 | tf_op jit(solution)/shard_map/td,ktc->kdc/dot_general | solution.py:53
  216.2 15.2 %fusion.37 = f32[2,512,512]{1,2,0:T(8,128)S(1)} fusion(bf16[512,4096]{1,0:T(8,128)(2,1)} %all-gather.2.cloned.1.call-done, f32[2,512,4096]{2,1,0:T(8,128)} %fusion.19, bf16[2,4096,512]{1,2,0:T(8,128)(2,1)S(1)} %bitcast.159), kind=kOutput, calls=%fused_computation.46 | convolution fusion | flops 4341104640 | bytes 31457280 | tf_op jit(solution)/shard_map/td,kdc->ktc/dot_general | solution.py:44
  231.4 0.6 multiply_bitcast_fusion.1
  232.0 39.7 %fusion.2 = bf16[2,4096,512]{1,2,0:T(8,128)(2,1)} fusion(bf16[2,4096,512]{1,2,0:T(8,128)(2,1)S(1)} %bitcast.159, f32[2,512,4096]{2,1,0:T(8,128)} %fusion.19, bf16[512,4096]{1,0:T(8,128)(2,1)} %all-gather.2.cloned.1.call-done, f32[1,512,512]{1,2,0:T(8,128)S(1)} %get-tuple-element.12, f32[1,512,512]{1,2,0:T(8,128)S(1)} %get-tuple-element.11), kind=kOutput, calls=%fused_computation.9 | convolution fusion | flops 25883574272 | bytes 39845888 | tf_op jit(solution)/shard_map/td,ktc->kdc/dot_general | solution.py:53
  271.6 12.0 %copy.36 = bf16[2,4096,512]{2,1,0:T(8,128)(2,1)} copy(bf16[2,4096,512]{1,2,0:T(8,128)(2,1)} %fusion.2) | data formatting | bytes 16777216 | tf_op jit(solution)/shard_map/convert_element_type | solution.py:62
  283.6 8.3 %copy.37 = bf16[128,2,32,512]{3,2,1,0:T(8,128)(2,1)} copy(bf16[128,2,32,512]{3,2,0,1:T(8,128)(2,1)} %bitcast.156) | data formatting | bytes 16777216 | tf_op jit(solution)/shard_map/reshape | solution.py:66
  291.9 6.2 %all-to-all-start.1 = ((bf16[128,2,32,512]{3,2,1,0:T(8,128)(2,1)}), bf16[128,2,32,512]{3,2,1,0:T(8,128)(2,1)}, u32[]{:S(2)}, u32[]{:S(2)}) async-start(bf16[128,2,32,512]{3,2,1,0:T(8,128)(2,1)} %copy.37), calls=%async_computation.1 | async-start | bytes 16777216 | tf_op jit(solution)/shard_map/all_to_all | solution.py:67
  298.2 0.1 convert_reduce_fusion
  298.3 98.9 %all-to-all-done.1 = bf16[128,2,32,512]{3,2,1,0:T(8,128)(2,1)} async-done(((bf16[128,2,32,512]{3,2,1,0:T(8,128)(2,1)}), bf16[128,2,32,512]{3,2,1,0:T(8,128)(2,1)}, u32[]{:S(2)}, u32[]{:S(2)}) %all-to-all-start.1) | async-done | bytes 8388640 | tf_op jit(solution)/shard_map/all_to_all | solution.py:67
  397.2 11.4 %copy.38 = bf16[16,2,32,8,512]{4,3,1,0,2:T(8,128)(2,1)} copy(bf16[16,2,32,8,512]{4,2,1,3,0:T(8,128)(2,1)} %bitcast.24) | data formatting | bytes 16777216 | tf_op jit(solution)/shard_map/transpose | solution.py:94
  408.6 13.5 %reshape.63 = bf16[32,32,4096]{2,0,1:T(8,128)(2,1)} reshape(bf16[16,2,32,8,512]{4,3,1,0,2:T(8,128)(2,1)} %copy.38) | data formatting | bytes 16777216 | tf_op jit(solution)/shard_map/reshape | solution.py:94
  422.1 19.0 %subtract_convert_fusion = (bf16[16,32,4096]{2,0,1:T(8,128)(2,1)S(1)}, bf16[16,32,4096]{2,0,1:T(8,128)(2,1)}) fusion(bf16[16,32,4096]{2,1,0:T(8,128)(2,1)} %param.9, bf16[16,32,4096]{2,1,0:T(8,128)(2,1)} %param.10, f32[16]{0:T(128)S(1)} %convert_reduce_fusion, bf16[32,32,4096]{2,0,1:T(8,128)(2,1)} %reshape.63, s32[32]{0:T(128)S(1)} %copy-done.6), kind=kOutput, calls=%fused_computation.21 | convolution fusion | flops 157286912 | bytes 25166016 | tf_op jit(solution)/shard_map/ms,srw->mrw/dot_general | solution.py:97
  441.1 4.3 copy.40
  445.4 7.5 %gather_fusion.1 = bf16[32,32,4096]{2,1,0:T(8,128)(2,1)} fusion(bf16[16,32,4096]{2,1,0:T(8,128)(2,1)} %copy.40, s32[1024]{0:T(1024)} %copy-done.2), kind=kCustom, calls=%fused_computation.1.clone | custom fusion | bytes 16777344 | tf_op jit(solution)/shard_map/jit(_take)/gather | solution.py:81
  452.9 7.5 %broadcast_select_fusion = bf16[32,32,4096]{2,1,0:T(8,128)(2,1)} fusion(bf16[32,32,4096]{2,1,0:T(8,128)(2,1)} %gather_fusion.1, pred[32]{0:T(512)(128)(4,1)S(1)} %copy-done.4), kind=kLoop, calls=%fused_computation.26 | loop fusion | flops 4194304 | bytes 16777248 | tf_op jit(solution)/shard_map/jit(_take)/select_n | solution.py:81
  460.4 12.2 %copy.49 = bf16[128,8,8,512]{3,2,1,0:T(8,128)(2,1)} copy(bf16[128,8,8,512]{3,1,2,0:T(8,128)(2,1)} %bitcast.149) | data formatting | bytes 16777216
  472.6 10.2 %copy.41 = bf16[16,2,32,8,512]{4,2,1,3,0:T(8,128)(2,1)} copy(bf16[16,2,32,8,512]{4,3,2,1,0:T(8,128)(2,1)} %bitcast.157) | data formatting | bytes 16777216 | tf_op jit(solution)/shard_map/reshape | solution.py:81
  482.7 12.7 %all-to-all-start.2 = ((bf16[128,2,32,512]{3,2,1,0:T(8,128)(2,1)}), bf16[128,2,32,512]{3,2,1,0:T(8,128)(2,1)}, u32[]{:S(2)}, u32[]{:S(2)}) async-start(bf16[128,2,32,512]{3,2,1,0:T(8,128)(2,1)} %bitcast.152), calls=%async_computation.2 | async-start | bytes 16777216 | tf_op jit(solution)/shard_map/all_to_all | solution.py:67
  495.5 6.5 %copy.44 = bf16[16,32,4096]{2,1,0:T(8,128)(2,1)} copy(bf16[16,32,4096]{2,0,1:T(8,128)(2,1)} %get-tuple-element.10) | data formatting | bytes 8388608
  502.0 92.4 %all-to-all-done.2 = bf16[128,2,32,512]{3,2,1,0:T(8,128)(2,1)} async-done(((bf16[128,2,32,512]{3,2,1,0:T(8,128)(2,1)}), bf16[128,2,32,512]{3,2,1,0:T(8,128)(2,1)}, u32[]{:S(2)}, u32[]{:S(2)}) %all-to-all-start.2) | async-done | bytes 8388640 | tf_op jit(solution)/shard_map/all_to_all | solution.py:67
  594.4 8.4 %copy.42 = bf16[16,8,2,32,512]{4,3,1,0,2:T(8,128)(2,1)} copy(bf16[16,8,2,32,512]{4,3,2,1,0:T(8,128)(2,1)} %bitcast.27) | data formatting | bytes 16777216 | tf_op jit(solution)/shard_map/reshape | solution.py:68
  602.8 7.1 %fusion.34 = f32[2,512,512]{1,2,0:T(8,128)S(1)} fusion(bf16[2,4096,512]{2,1,0:T(8,128)(2,1)} %bitcast.160, bf16[512,4096]{1,0:T(8,128)(2,1)S(1)} %copy-done.8), kind=kOutput, calls=%fused_computation.45 | convolution fusion | flops 4294967296 | bytes 14680064 | tf_op jit(solution)/shard_map/td,kdc->ktc/dot_general | solution.py:106
  609.9 0.3 fusion.47
  610.2 1.0 copy.45
  (21 shorter events, 0.1 us)
Async XLA Ops:
  8.0 7.3 %copy-start.5 = (s32[32]{0:T(128)}, s32[32]{0:T(128)S(1)}, u32[]{:S(2)}) copy-start(s32[32]{0:T(128)S(1)} %eq.15) | copy-start | bytes 388
  8.0 7.3 %copy-start.3 = (pred[32]{0:T(512)(128)(4,1)}, pred[32]{0:T(512)(128)(4,1)S(1)}, u32[]{:S(2)}) copy-start(pred[32]{0:T(512)(128)(4,1)S(1)} %compare_and_fusion) | copy-start | bytes 100
  8.1 7.2 %copy-start.2 = (s32[1024]{0:T(1024)}, s32[1024]{0:T(1024)S(1)}, u32[]{:S(2)}) copy-start(s32[1024]{0:T(1024)S(1)} %pad_clamp_fusion) | copy-start | bytes 12292
  45.1 12.0 %copy-start = (bf16[64,4096]{1,0:T(8,128)(2,1)S(1)}, bf16[64,4096]{1,0:T(8,128)(2,1)}, u32[]{:S(2)}) copy-start(bf16[64,4096]{1,0:T(8,128)(2,1)} %param.7) | copy-start | bytes 1572868
  45.1 13.2 %copy-start.1 = (bf16[512,512]{1,0:T(8,128)(2,1)S(1)}, bf16[512,512]{1,0:T(8,128)(2,1)}, u32[]{:S(2)}) copy-start(bf16[512,512]{1,0:T(8,128)(2,1)} %param.8) | copy-start | bytes 1572868
  45.1 126.7 %all-to-all-start = ((bf16[128,2,32,512]{3,2,1,0:T(8,128)(2,1)}), bf16[128,2,32,512]{3,2,1,0:T(8,128)(2,1)}, u32[]{:S(2)}, u32[]{:S(2)}) async-start(bf16[128,2,32,512]{3,2,1,0:T(8,128)(2,1)} %bitcast.151), calls=%async_computation | async-start | bytes 16777216 | tf_op jit(solution)/shard_map/all_to_all | solution.py:67
  57.1 134.3 %all-gather.2.cloned.1.call-start = ((), (), s32[]{:S(2)}) async-start(), calls=%async_computation.3 | async-start | bytes 4718592 | tf_op jit(solution)/shard_map/all_gather | solution.py:78
  191.4 9.0 %copy-start.7 = (bf16[512,4096]{1,0:T(8,128)(2,1)S(1)}, bf16[512,4096]{1,0:T(8,128)(2,1)}, u32[]{:S(2)}) copy-start(bf16[512,4096]{1,0:T(8,128)(2,1)} %all-gather.2.cloned.1.call-done) | copy-start | bytes 12582916
  199.8 16.4 %slice-start = ((s8[8388608]{0:T(1024)(128)(4,1)}), s8[4194304]{0:T(1024)(128)(4,1)S(1)}, s32[]{:S(2)}) async-start(s8[8388608]{0:T(1024)(128)(4,1)} %bitcast.158), calls=%async_computation.4 | async-start | bytes 8388608
  200.4 15.8 %slice-start.1 = ((s8[8388608]{0:T(1024)(128)(4,1)}), s8[4194304]{0:T(1024)(128)(4,1)S(1)}, s32[]{:S(2)}) async-start(s8[8388608]{0:T(1024)(128)(4,1)} %bitcast.158), calls=%async_computation.5 | async-start | bytes 8388608
  291.9 6.3 %copy-start.6 = (s32[32]{0:T(128)S(1)}, s32[32]{0:T(128)}, u32[]{:S(2)}) copy-start(s32[32]{0:T(128)} %copy-done.5) | copy-start | bytes 388
  291.9 105.3 %all-to-all-start.1 = ((bf16[128,2,32,512]{3,2,1,0:T(8,128)(2,1)}), bf16[128,2,32,512]{3,2,1,0:T(8,128)(2,1)}, u32[]{:S(2)}, u32[]{:S(2)}) async-start(bf16[128,2,32,512]{3,2,1,0:T(8,128)(2,1)} %copy.37), calls=%async_computation.1 | async-start | bytes 16777216 | tf_op jit(solution)/shard_map/all_to_all | solution.py:67
  445.4 7.5 %copy-start.4 = (pred[32]{0:T(512)(128)(4,1)S(1)}, pred[32]{0:T(512)(128)(4,1)}, u32[]{:S(2)}) copy-start(pred[32]{0:T(512)(128)(4,1)} %copy-done.3) | copy-start | bytes 100
  482.7 111.6 %all-to-all-start.2 = ((bf16[128,2,32,512]{3,2,1,0:T(8,128)(2,1)}), bf16[128,2,32,512]{3,2,1,0:T(8,128)(2,1)}, u32[]{:S(2)}, u32[]{:S(2)}) async-start(bf16[128,2,32,512]{3,2,1,0:T(8,128)(2,1)} %bitcast.152), calls=%async_computation.2 | async-start | bytes 16777216 | tf_op jit(solution)/shard_map/all_to_all | solution.py:67
  594.4 8.4 %copy-start.8 = (bf16[512,4096]{1,0:T(8,128)(2,1)S(1)}, bf16[512,4096]{1,0:T(8,128)(2,1)}, u32[]{:S(2)}) copy-start(bf16[512,4096]{1,0:T(8,128)(2,1)} %all-gather.2.cloned.1.call-done) | copy-start | bytes 12582916
Sparse Core Ops, SparseCore 0:
  60.2 67.9 all-gather.1
where the time goes:
time: 630 us; the launch traced here: 618 us
  waiting for transfers between devices  305 us (48%)
  local copies, waits for them, and re-layouts  145 us (23%)
  matrix products  105 us (17%)
  starting transfers between devices  31 us (5%)
  other arithmetic  17.8 us (3%)
  between operations  14.5 us (2%)
    all_to_all x3, waiting for transfers between devices, move_blocks(): lax.all_to_all(flattened, ('path', 'mp'), split_axis=0, concat_axis=0, ti...  305 us
    dot_general x2, matrix products, path_round(): jnp.einsum('td,ktc->kdc', wide, slopes, precision=lax.Precision.HIGHEST,...  55.5 us
    unnamed x28, local copies, waits for them, and re-layouts  32.9 us
    all_to_all x3, starting transfers between devices, move_blocks(): lax.all_to_all(flattened, ('path', 'mp'), split_axis=0, concat_axis=0, ti...  30.9 us
    dot_general x2, matrix products, path_round(): jnp.einsum('td,kdc->ktc', normed, current, preferred_element_type=jnp.flo...  23.6 us
    dot_general x1, matrix products, local(): jnp.einsum('ms,srw->mrw', select.astype(jnp.bfloat16), row_blocks, prefer...  19 us
    reshape x2, local copies, waits for them, and re-layouts, move_blocks(): return arrived.reshape(buffer.shape)  16.7 us
    select_n x3, other arithmetic, deliver(): jnp.take(table, flat_lists, axis=0)  15 us
  transfers between devices with their start and end apart: 4, of which 3 were waited for; matrix products, arithmetic and copies ran while one was open for 4% of the time, Pallas kernels for 0%

commit v1 on v0

v1 whole, which is shorter than its diff:
```python
import functools

import jax
import jax.numpy as jnp
from jax import lax
from jax.experimental import pallas as pl
from jax.experimental.pallas import tpu as pltpu
from jax.sharding import PartitionSpec as P

TOK_PATH = 512
beta_first = 0.9
beta_second = 0.95
adam_epsilon = 1e-05
inner_rate = 0.004
weight_decay = 0.1
outer_rate = 0.7
outer_momentum = 0.9
VMEM_LIMIT = 56 * 1024 * 1024

NT = (((1,), (1,)), ((), ()))


def normalize(features):
    values = features.astype(jnp.float32)
    factor = lax.rsqrt(jnp.mean(values * values, axis=-1, keepdims=True) + 1e-05)
    return (values * factor).astype(jnp.bfloat16)


def spread_kernel(table_ref, out_ref):
    for g in range(4):
        turned = table_ref[g].T
        out_ref[:, 0, g] = turned.reshape(out_ref.shape[0], out_ref.shape[3], 128)


def spread(table, paths, shards):
    modules, rows, width = table.shape
    groups = modules * rows // 128
    wide = width // shards
    cols = wide // paths
    return pl.pallas_call(
        spread_kernel,
        grid=(shards,),
        in_specs=[pl.BlockSpec((groups, 128, wide), lambda i: (0, 0, i))],
        out_specs=pl.BlockSpec((paths, 1, groups, cols, 128), lambda i: (0, i, 0, 0, 0)),
        out_shape=jax.ShapeDtypeStruct((paths, shards, groups, cols, 128), table.dtype),
        compiler_params=pltpu.CompilerParams(vmem_limit_bytes=VMEM_LIMIT),
        name="spread",
    )(table.reshape(groups, 128, width))


def unspread_kernel(blocks_ref, out_ref):
    for g in range(4):
        out_ref[g] = blocks_ref[:, 0, g].reshape(-1, 128).T


def unspread(blocks, modules, rows):
    paths, shards, groups, cols, _ = blocks.shape
    wide = paths * cols
    out = pl.pallas_call(
        unspread_kernel,
        grid=(shards,),
        in_specs=[pl.BlockSpec((paths, 1, groups, cols, 128), lambda i: (0, i, 0, 0, 0))],
        out_specs=pl.BlockSpec((groups, 128, wide), lambda i: (0, 0, i)),
        out_shape=jax.ShapeDtypeStruct((groups, 128, wide * shards), blocks.dtype),
        compiler_params=pltpu.CompilerParams(vmem_limit_bytes=VMEM_LIMIT),
        name="unspread",
    )(blocks)
    return out.reshape(modules, rows, wide * shards)


def swap_matrix():
    index = jnp.arange(512)
    source, module, row = index // 128, (index // 32) % 4, index % 32
    return (index[:, None] == (module * 128 + source * 32 + row)[None, :]).astype(jnp.bfloat16)


def gather_kernel(blocks_ref, swap_ref, out_ref):
    quads, cols = blocks_ref.shape[0] // 4, blocks_ref.shape[2]
    for k in range(quads):
        line = jnp.concatenate([blocks_ref[4 * k + s, 0] for s in range(4)], axis=1)
        turned = jnp.dot(line, swap_ref[...], preferred_element_type=jnp.float32).astype(jnp.bfloat16)
        for q in range(4):
            out_ref[q, :, k * 128 : (k + 1) * 128] = turned[:, q * 128 : (q + 1) * 128]


def gather_columns(blocks):
    devices, groups, cols, _ = blocks.shape
    return pl.pallas_call(
        gather_kernel,
        grid=(groups,),
        in_specs=[
            pl.BlockSpec((devices, 1, cols, 128), lambda g: (0, g, 0, 0)),
            pl.BlockSpec((512, 512), lambda g: (0, 0)),
        ],
        out_specs=pl.BlockSpec((4, cols, devices * 32), lambda g: (g, 0, 0)),
        out_shape=jax.ShapeDtypeStruct((groups * 4, cols, devices * 32), blocks.dtype),
        compiler_params=pltpu.CompilerParams(vmem_limit_bytes=VMEM_LIMIT),
        name="gather_columns",
    )(blocks, swap_matrix())


def scatter_kernel(table_ref, swap_ref, out_ref):
    quads = out_ref.shape[0] // 4
    for k in range(quads):
        line = jnp.concatenate([table_ref[q, :, k * 128 : (k + 1) * 128] for q in range(4)], axis=1)
        turned = jnp.dot(line, swap_ref[...], preferred_element_type=jnp.float32).astype(jnp.bfloat16)
        for s in range(4):
            out_ref[4 * k + s, 0] = turned[:, s * 128 : (s + 1) * 128]


def scatter_columns(table):
    modules, cols, width = table.shape
    groups, devices = modules // 4, width // 32
    return pl.pallas_call(
        scatter_kernel,
        grid=(groups,),
        in_specs=[
            pl.BlockSpec((4, cols, width), lambda g: (g, 0, 0)),
            pl.BlockSpec((512, 512), lambda g: (0, 0)),
        ],
        out_specs=pl.BlockSpec((devices, 1, cols, 128), lambda g: (0, g, 0, 0)),
        out_shape=jax.ShapeDtypeStruct((devices, groups, cols, 128), table.dtype),
        compiler_params=pltpu.CompilerParams(vmem_limit_bytes=VMEM_LIMIT),
        name="scatter_columns",
    )(table, swap_matrix())


def pieces(value):
    high = value.astype(jnp.bfloat16)
    rest = value - high.astype(jnp.float32)
    middle = rest.astype(jnp.bfloat16)
    low = (rest - middle.astype(jnp.float32)).astype(jnp.bfloat16)
    return jnp.concatenate([high, middle, low], axis=0)


def slopes(weights, normed, goal):
    cols = goal.shape[0]
    both = lax.dot_general(weights, normed, NT, preferred_element_type=jnp.float32)
    gate_act, up_act = both[:cols], both[cols:]
    sigma = jax.nn.sigmoid(gate_act)
    swish = gate_act * sigma
    error = (swish * up_act - goal) / TOK_PATH
    d_gate = error * up_act * sigma * (1.0 + gate_act * (1.0 - sigma))
    d_up = error * swish
    return pieces(jnp.concatenate([d_gate, d_up], axis=0))


TILE = 512


def inner_kernel(lists_ref, normed_ref, goal_ref, table_ref, sums_ref, start, current, first_grad, slope):
    path = pl.program_id(0)
    gate, up = lists_ref[2 * path], lists_ref[2 * path + 1]
    cols = goal_ref.shape[1]
    width = normed_ref.shape[1]

    @pl.when(path == 0)
    def _():
        sums_ref[...] = jnp.zeros_like(sums_ref)

    start[:cols] = table_ref[gate]
    start[cols:] = table_ref[up]
    goal = goal_ref[0].astype(jnp.float32)
    slope[...] = slopes(start[...], normed_ref[...], goal)

    def product(columns):
        parts = jnp.dot(slope[...], normed_ref[:, columns], preferred_element_type=jnp.float32)
        return parts[: 2 * cols] + (parts[2 * cols : 4 * cols] + parts[4 * cols :])

    def after_first(begin, grad):
        return begin - inner_rate * (grad / (jnp.abs(grad) + adam_epsilon) + weight_decay * begin)

    for j in range(width // TILE):
        columns = slice(j * TILE, (j + 1) * TILE)
        grad = product(columns)
        first_grad[:, columns] = grad
        begin = start[:, columns].astype(jnp.float32)
        current[:, columns] = after_first(begin, grad).astype(jnp.bfloat16)

    slope[...] = slopes(current[...], normed_ref[...], goal)
    for j in range(width // TILE):
        columns = slice(j * TILE, (j + 1) * TILE)
        grad = product(columns)
        before = first_grad[:, columns]
        begin = start[:, columns].astype(jnp.float32)
        master = after_first(begin, before)
        first = (beta_first * (1.0 - beta_first) / (1.0 - beta_first**2)) * before + (
            (1.0 - beta_first) / (1.0 - beta_first**2)
        ) * grad
        second = (beta_second * (1.0 - beta_second) / (1.0 - beta_second**2)) * before * before + (
            (1.0 - beta_second) / (1.0 - beta_second**2)
        ) * grad * grad
        master = master - inner_rate * (
            first / (jnp.sqrt(second) + adam_epsilon) + weight_decay * master
        )
        delta = (begin - master).astype(jnp.bfloat16).astype(jnp.float32)
        sums_ref[gate, :, columns] += delta[:cols]
        sums_ref[up, :, columns] += delta[cols:]


def inner_steps(lists, normed, goals, table):
    modules, cols, width = table.shape
    paths = goals.shape[0]
    tokens = normed.shape[0]
    return pl.pallas_call(
        inner_kernel,
        grid_spec=pltpu.PrefetchScalarGridSpec(
            num_scalar_prefetch=1,
            grid=(paths,),
            in_specs=[
                pl.BlockSpec((TOK_PATH, width), lambda p, s: (p, 0)),
                pl.BlockSpec((1, cols, TOK_PATH), lambda p, s: (p, 0, 0)),
                pl.BlockSpec((modules, cols, width), lambda p, s: (0, 0, 0)),
            ],
            out_specs=pl.BlockSpec((modules, cols, width), lambda p, s: (0, 0, 0)),
            scratch_shapes=[
                pltpu.VMEM((2 * cols, width), jnp.bfloat16),
                pltpu.VMEM((2 * cols, width), jnp.bfloat16),
                pltpu.VMEM((2 * cols, width), jnp.float32),
                pltpu.VMEM((6 * cols, TOK_PATH), jnp.bfloat16),
            ],
        ),
        out_shape=jax.ShapeDtypeStruct((modules, cols, width), jnp.float32),
        compiler_params=pltpu.CompilerParams(vmem_limit_bytes=VMEM_LIMIT),
        cost_estimate=pl.CostEstimate(
            flops=32 * tokens * width * cols, bytes_accessed=2 * tokens * width, transcendentals=0
        ),
        name="inner_steps",
    )(lists, normed, goals, table)


def evaluate_kernel(lists_ref, normed_ref, table_ref, out_ref, weights):
    path = pl.program_id(0)
    cols = out_ref.shape[1]
    weights[:cols] = table_ref[lists_ref[2 * path]]
    weights[cols:] = table_ref[lists_ref[2 * path + 1]]
    both = lax.dot_general(weights[...], normed_ref[...], NT, preferred_element_type=jnp.float32)
    gate_act = both[:cols]
    out_ref[0] = (gate_act * jax.nn.sigmoid(gate_act) * both[cols:]).astype(jnp.bfloat16)


def evaluate(lists, normed, table):
    modules, cols, width = table.shape
    tokens = normed.shape[0]
    paths = tokens // TOK_PATH
    return pl.pallas_call(
        evaluate_kernel,
        grid_spec=pltpu.PrefetchScalarGridSpec(
            num_scalar_prefetch=1,
            grid=(paths,),
            in_specs=[
                pl.BlockSpec((TOK_PATH, width), lambda p, s: (p, 0)),
                pl.BlockSpec((modules, cols, width), lambda p, s: (0, 0, 0)),
            ],
            out_specs=pl.BlockSpec((1, cols, TOK_PATH), lambda p, s: (p, 0, 0)),
            scratch_shapes=[pltpu.VMEM((2 * cols, width), jnp.bfloat16)],
        ),
        out_shape=jax.ShapeDtypeStruct((paths, cols, TOK_PATH), jnp.bfloat16),
        compiler_params=pltpu.CompilerParams(vmem_limit_bytes=VMEM_LIMIT),
        cost_estimate=pl.CostEstimate(
            flops=4 * tokens * width * cols, bytes_accessed=2 * tokens * width, transcendentals=0
        ),
        name="evaluate",
    )(lists, normed, table)


def exchange(blocks, axes):
    return lax.all_to_all(blocks, axes, split_axis=0, concat_axis=0, tiled=True)


def local(features, targets, module_table, momentum, path_lists):
    paths = lax.axis_size("path")
    shards = lax.axis_size("mp")
    modules, rows_own, width = module_table.shape
    cols = width // (paths * shards)
    lists = path_lists.reshape(-1)
    both = ("path", "mp")

    def to_columns(table):
        blocks = spread(table, paths, shards)
        blocks = blocks.reshape((paths * shards,) + blocks.shape[2:])
        return gather_columns(exchange(blocks, both))

    def to_rows(table):
        blocks = exchange(scatter_columns(table), both)
        return unspread(blocks.reshape((paths, shards) + blocks.shape[1:]), modules, rows_own)

    normed = lax.all_gather(normalize(features), both, axis=0, tiled=True)
    table = to_columns(module_table)
    goals = exchange(targets.T.reshape(paths, cols, TOK_PATH), "path")
    speed = to_columns(momentum)
    sums = inner_steps(lists, normed, goals, table)
    select = lists[None, :] == jnp.arange(modules, dtype=jnp.int32)[:, None]
    counts = jnp.sum(select.astype(jnp.float32), axis=1)
    average = sums / counts[:, None, None]
    moment = outer_momentum * speed.astype(jnp.float32) + average
    updated = (
        table.astype(jnp.float32) - outer_rate * (average + outer_momentum * moment)
    ).astype(jnp.bfloat16)
    momentum_out = to_rows(moment.astype(jnp.bfloat16))
    evaluated = evaluate(lists, normed, updated)
    evaluated = exchange(evaluated, "path").reshape(paths * cols, TOK_PATH).T
    return (momentum_out, evaluated)


def solution(mesh):
    return jax.shard_map(
        local,
        mesh=mesh,
        in_specs=(
            P(("path", "mp"), None),
            P("path", "mp"),
            P(None, ("path", "mp"), None),
            P(None, ("path", "mp"), None),
            P(),
        ),
        out_specs=(P(None, ("path", "mp"), None), P("path", "mp")),
        check_vma=False,
    )
```

time: 630 us -> 496 us (0.79); the launches traced: 618 us -> 494 us
  Pallas kernels: 0 us -> 190 us
  local copies, waits for them, and re-layouts: 145 us -> 2.24 us
  matrix products: 105 us -> 0 us
  waiting for transfers between devices: 305 us -> 241 us
    pallas_call x0 -> x8, Pallas kernels: none -> 190 us  [the longest x1 90.6 us: inner_steps(): pl.pallas_call(inner_kernel, grid_spec=pltpu.PrefetchScalarGridSpec(num_s...]
    all_to_all x3 -> x5, waiting for transfers between devices: 305 us -> 169 us  [exchange(): return lax.all_to_all(blocks, axes, split_axis=0, concat_axis=0, tiled=True)]
    dot_general x6 -> x0, matrix products: 105 us -> none  [the longest x2 55.5 us: path_round(): jnp.einsum('td,ktc->kdc', wide, slopes, precision=lax.Precision.HIGHEST,...]
    all_gather x1, waiting for transfers between devices: 0.01 us -> 72.2 us  [local(): normed = lax.all_gather(normalize(features), both, axis=0, tiled=True)]
    reshape x6 -> x2, local copies, waits for them, and re-layouts: 59.9 us -> 1.09 us  [the longest x1 1 us: local(): evaluated = exchange(evaluated, 'path').reshape(paths * cols, TOK_PATH).T]
    unnamed x28 -> x11, local copies, waits for them, and re-layouts: 32.9 us -> 0.1 us
    transpose x2 -> x1, local copies, waits for them, and re-layouts: 21.5 us -> 1.04 us  [local(): goals = exchange(targets.T.reshape(paths, cols, TOK_PATH), 'path')]
    convert_element_type x2 -> x0, local copies, waits for them, and re-layouts: 16.3 us -> none  [the longest x1 12 us: path_round(): return (start.astype(jnp.float32) - master).astype(jnp.bfloat16)]
  transfers between devices with their start and end apart: 4 -> 6, of which waited for: 3 -> 4; matrix products, arithmetic and copies ran while one was open for 4% -> 1% of each run, Pallas kernels for 0% -> 12%
where the time goes in v1:
time: 496 us; the launch traced here: 494 us
  waiting for transfers between devices  241 us (49%)
  Pallas kernels  190 us (38%)
  starting transfers between devices  34 us (7%)
  between operations  14.1 us (3%)
  other arithmetic  12.5 us (3%)
    all_to_all x5, waiting for transfers between devices, exchange(): return lax.all_to_all(blocks, axes, split_axis=0, concat_axis=0, tiled=True)  169 us
    pallas_call x1, Pallas kernels, inner_steps(): pl.pallas_call(inner_kernel, grid_spec=pltpu.PrefetchScalarGridSpec(num_s...  90.6 us
    all_gather x1, waiting for transfers between devices, local(): normed = lax.all_gather(normalize(features), both, axis=0, tiled=True)  72.2 us
    all_to_all x5, starting transfers between devices, exchange(): return lax.all_to_all(blocks, axes, split_axis=0, concat_axis=0, tiled=True)  33.9 us
    pallas_call x1, Pallas kernels, evaluate(): pl.pallas_call(evaluate_kernel, grid_spec=pltpu.PrefetchScalarGridSpec(nu...  33.7 us
    pallas_call x2, Pallas kernels, gather_columns(): pl.pallas_call(gather_kernel, grid=(groups,), in_specs=[pl.BlockSpec((dev...  30.2 us
    pallas_call x2, Pallas kernels, spread(): pl.pallas_call(spread_kernel, grid=(shards,), in_specs=[pl.BlockSpec((gro...  14.4 us
    pallas_call x1, Pallas kernels, scatter_columns(): pl.pallas_call(scatter_kernel, grid=(groups,), in_specs=[pl.BlockSpec((4,...  14.3 us
  transfers between devices with their start and end apart: 6, of which 4 were waited for; matrix products, arithmetic and copies ran while one was open for 1% of the time, Pallas kernels for 12%

profile of v1, /device:TPU:1, one launch (start us, length us, event | category | flops | bytes accessed | tf_op | source)
XLA Modules:
  0.0 494.3 jit_solution(5546012468205313912)
XLA Ops:
  7.2 0.0 all-gather.2.cloned.1.call-start
  7.2 1.2 fusion.1
  8.5 2.0 fusion.2
  10.5 0.0 all-gather.2.cloned.1.call-update
  10.5 7.2 %spread.3 = bf16[16,8,4,32,128]{4,3,2,1,0:T(8,128)(2,1)} custom-call(bf16[4,128,4096]{2,1,0:T(8,128)(2,1)} %bitcast.12), custom_call_target="tpu_custom_call" | custom-call | tf_op jit(solution)/shard_map/spread/pallas_call | solution.py:40
  17.7 12.0 %all-to-all-start.2 = ((bf16[128,4,32,128]{3,2,1,0:T(8,128)(2,1)}), bf16[128,4,32,128]{3,2,1,0:T(8,128)(2,1)}, u32[]{:S(2)}, u32[]{:S(2)}) async-start(bf16[128,4,32,128]{3,2,1,0:T(8,128)(2,1)} %bitcast.11), calls=%async_computation.2 | async-start | bytes 8388608 | tf_op jit(solution)/shard_map/all_to_all | solution.py:268
  29.7 7.2 %spread.2 = bf16[16,8,4,32,128]{4,3,2,1,0:T(8,128)(2,1)} custom-call(bf16[4,128,4096]{2,1,0:T(8,128)(2,1)} %bitcast.13), custom_call_target="tpu_custom_call" | custom-call | tf_op jit(solution)/shard_map/spread/pallas_call | solution.py:40
  36.9 48.6 %all-to-all-done.2.blocks_ref = bf16[128,4,32,128]{3,2,1,0:T(8,128)(2,1)} async-done(((bf16[128,4,32,128]{3,2,1,0:T(8,128)(2,1)}), bf16[128,4,32,128]{3,2,1,0:T(8,128)(2,1)}, u32[]{:S(2)}, u32[]{:S(2)}) %all-to-all-start.2) | async-done | bytes 4194336 | tf_op jit(solution)/shard_map/all_to_all | solution.py:268
  85.5 0.0 copy-start.1
  85.5 0.0 copy-start.4
  85.5 5.5 %all-to-all-start = ((bf16[128,4,32,128]{3,2,1,0:T(8,128)(2,1)}), bf16[128,4,32,128]{3,2,1,0:T(8,128)(2,1)}, u32[]{:S(2)}, u32[]{:S(2)}) async-start(bf16[128,4,32,128]{3,2,1,0:T(8,128)(2,1)} %bitcast.10), calls=%async_computation | async-start | bytes 8388608 | tf_op jit(solution)/shard_map/all_to_all | solution.py:268
  91.0 0.0 copy-done.1
  91.0 1.0 copy.14
  92.1 68.8 %all-to-all-done.blocks_ref = bf16[128,4,32,128]{3,2,1,0:T(8,128)(2,1)} async-done(((bf16[128,4,32,128]{3,2,1,0:T(8,128)(2,1)}), bf16[128,4,32,128]{3,2,1,0:T(8,128)(2,1)}, u32[]{:S(2)}, u32[]{:S(2)}) %all-to-all-start) | async-done | bytes 4194336 | tf_op jit(solution)/shard_map/all_to_all | solution.py:268
  160.8 3.8 all-to-all-start.1
  164.6 0.0 copy-done.4
  164.6 0.1 copy.13
  164.7 0.1 reshape.86.lists_ref
  164.8 0.0 copy-start.3
  164.8 0.1 convert_reduce_fusion
  164.9 0.9 fusion.3.swap_ref
  165.8 15.0 %gather_columns.3.table_ref = bf16[16,32,4096]{2,1,0:T(8,128)(2,1)} custom-call(bf16[128,4,32,128]{3,2,1,0:T(8,128)(2,1)} %all-to-all-done.2.blocks_ref, bf16[512,512]{1,0:T(8,128)(2,1)} %fusion.3.swap_ref), custom_call_target="tpu_custom_call" | custom-call | tf_op jit(solution)/shard_map/gather_columns/pallas_call | solution.py:88
  180.9 0.0 copy-done.3
  180.9 15.1 %gather_columns.2 = bf16[16,32,4096]{2,1,0:T(8,128)(2,1)} custom-call(bf16[128,4,32,128]{3,2,1,0:T(8,128)(2,1)} %all-to-all-done.blocks_ref, bf16[512,512]{1,0:T(8,128)(2,1)} %fusion.3.swap_ref), custom_call_target="tpu_custom_call" | custom-call | tf_op jit(solution)/shard_map/gather_columns/pallas_call | solution.py:88
  196.0 0.0 all-to-all-done.1.goal_ref
  196.0 0.0 copy-start.2
  196.0 72.2 %all-gather.2.cloned.1.call-done.normed_ref = bf16[8192,4096]{1,0:T(8,128)(2,1)} async-done(((bf16[64,4096]{1,0:T(8,128)(2,1)}), bf16[8192,4096]{1,0:T(8,128)(2,1)}) %all-gather.2.cloned.1.call-update) | async-done | bytes 67108880 | tf_op jit(solution)/shard_map/all_gather | solution.py:288
  268.2 0.0 copy-done.2
  268.2 0.0 copy-start
  268.2 90.6 %inner_steps.1 = f32[16,32,4096]{2,1,0:T(8,128)} custom-call(s32[32]{0:T(128)} %copy-done.3, bf16[8192,4096]{1,0:T(8,128)(2,1)} %all-gather.2.cloned.1.call-done.normed_ref, bf16[16,32,512]{2,1,0:T(8,128)(2,1)} %copy-done.2, bf16[16,32,4096]{2,1,0:T(8,128)(2,1)} %gather_columns.3.table_ref), custom_call_target="tpu_custom_call" | custom-call | flops 34359738368 | bytes 67108864 | tf_op jit(solution)/shard_map/inner_steps/pallas_call | solution.py:205
  358.8 0.0 copy-done
  358.8 8.2 %subtract_convert_fusion = (bf16[16,32,4096]{2,1,0:T(8,128)(2,1)}, bf16[16,32,4096]{2,1,0:T(8,128)(2,1)}) fusion(bf16[16,32,4096]{2,1,0:T(8,128)(2,1)S(1)} %copy-done, bf16[16,32,4096]{2,1,0:T(8,128)(2,1)} %gather_columns.2, f32[16,32,4096]{2,1,0:T(8,128)} %inner_steps.1, f32[16]{0:T(128)S(1)} %convert_reduce_fusion), kind=kLoop, calls=%fused_computation | loop fusion | flops 23068672 | bytes 25165888 | tf_op jit(solution)/shard_map/convert_element_type | solution.py:299
  367.0 33.7 %evaluate.1 = bf16[16,32,512]{2,1,0:T(8,128)(2,1)} custom-call(s32[32]{0:T(128)} %copy-done.3, bf16[8192,4096]{1,0:T(8,128)(2,1)} %all-gather.2.cloned.1.call-done.normed_ref, bf16[16,32,4096]{2,1,0:T(8,128)(2,1)} %get-tuple-element.2.table_ref), custom_call_target="tpu_custom_call" | custom-call | flops 4294967296 | bytes 67108864 | tf_op jit(solution)/shard_map/evaluate/pallas_call | solution.py:246
  400.7 4.6 all-to-all-start.4
  405.2 14.3 %scatter_columns.1 = bf16[128,4,32,128]{3,2,1,0:T(8,128)(2,1)} custom-call(bf16[16,32,4096]{2,1,0:T(8,128)(2,1)} %get-tuple-element.3.table_ref, bf16[512,512]{1,0:T(8,128)(2,1)} %fusion.3.swap_ref), custom_call_target="tpu_custom_call" | custom-call | tf_op jit(solution)/shard_map/scatter_columns/pallas_call | solution.py:114
  419.6 0.0 all-to-all-done.4
  419.6 8.1 %all-to-all-start.3 = ((bf16[128,4,32,128]{3,2,1,0:T(8,128)(2,1)}), bf16[128,4,32,128]{3,2,1,0:T(8,128)(2,1)}, u32[]{:S(2)}, u32[]{:S(2)}) async-start(bf16[128,4,32,128]{3,2,1,0:T(8,128)(2,1)} %scatter_columns.1), calls=%async_computation.3 | async-start | bytes 8388608 | tf_op jit(solution)/shard_map/all_to_all | solution.py:268
  427.7 1.0 copy.15
  428.7 51.6 %all-to-all-done.3 = bf16[128,4,32,128]{3,2,1,0:T(8,128)(2,1)} async-done(((bf16[128,4,32,128]{3,2,1,0:T(8,128)(2,1)}), bf16[128,4,32,128]{3,2,1,0:T(8,128)(2,1)}, u32[]{:S(2)}, u32[]{:S(2)}) %all-to-all-start.3) | async-done | bytes 4194336 | tf_op jit(solution)/shard_map/all_to_all | solution.py:268
  480.3 7.2 %unspread.1 = bf16[4,128,4096]{2,1,0:T(8,128)(2,1)} custom-call(bf16[16,8,4,32,128]{4,3,2,1,0:T(8,128)(2,1)} %bitcast.6.blocks_ref), custom_call_target="tpu_custom_call" | custom-call | tf_op jit(solution)/shard_map/unspread/pallas_call | solution.py:59
  (2 shorter events, 0.0 us)
Async XLA Ops:
  7.2 261.0 %all-gather.2.cloned.1.call-start = ((), (), s32[]{:S(2)}) async-start(), calls=%async_computation.5 | async-start | bytes 67633152 | tf_op jit(solution)/shard_map/all_gather | solution.py:288
  17.7 67.7 %all-to-all-start.2 = ((bf16[128,4,32,128]{3,2,1,0:T(8,128)(2,1)}), bf16[128,4,32,128]{3,2,1,0:T(8,128)(2,1)}, u32[]{:S(2)}, u32[]{:S(2)}) async-start(bf16[128,4,32,128]{3,2,1,0:T(8,128)(2,1)} %bitcast.11), calls=%async_computation.2 | async-start | bytes 8388608 | tf_op jit(solution)/shard_map/all_to_all | solution.py:268
  85.5 5.6 %copy-start.1 = (bf16[512,512]{1,0:T(8,128)(2,1)S(1)}, bf16[512,512]{1,0:T(8,128)(2,1)}, u32[]{:S(2)}) copy-start(bf16[512,512]{1,0:T(8,128)(2,1)} %param.6) | copy-start | bytes 1572868
  85.5 79.1 %copy-start.4 = (s32[16,2]{0,1:T(2,128)S(1)}, s32[16,2]{0,1:T(2,128)}, u32[]{:S(2)}) copy-start(s32[16,2]{0,1:T(2,128)} %param.9) | copy-start | bytes 388
  85.5 75.4 %all-to-all-start = ((bf16[128,4,32,128]{3,2,1,0:T(8,128)(2,1)}), bf16[128,4,32,128]{3,2,1,0:T(8,128)(2,1)}, u32[]{:S(2)}, u32[]{:S(2)}) async-start(bf16[128,4,32,128]{3,2,1,0:T(8,128)(2,1)} %bitcast.10), calls=%async_computation | async-start | bytes 8388608 | tf_op jit(solution)/shard_map/all_to_all | solution.py:268
  160.8 35.2 %all-to-all-start.1 = ((bf16[16,32,512]{2,1,0:T(8,128)(2,1)}), bf16[16,32,512]{2,1,0:T(8,128)(2,1)S(1)}, u32[]{:S(2)}, u32[]{:S(2)}) async-start(bf16[16,32,512]{2,1,0:T(8,128)(2,1)} %bitcast.3), calls=%async_computation.1 | async-start | bytes 1048576 | tf_op jit(solution)/shard_map/all_to_all | solution.py:268
  164.8 16.1 %copy-start.3 = (s32[32]{0:T(128)}, s32[32]{0:T(128)S(1)}, u32[]{:S(2)}) copy-start(s32[32]{0:T(128)S(1)} %reshape.86.lists_ref) | copy-start | bytes 388
  196.0 72.2 %copy-start.2 = (bf16[16,32,512]{2,1,0:T(8,128)(2,1)}, bf16[16,32,512]{2,1,0:T(8,128)(2,1)S(1)}, u32[]{:S(2)}) copy-start(bf16[16,32,512]{2,1,0:T(8,128)(2,1)S(1)} %all-to-all-done.1.goal_ref) | copy-start | bytes 1572868
  268.2 90.6 %copy-start = (bf16[16,32,4096]{2,1,0:T(8,128)(2,1)S(1)}, bf16[16,32,4096]{2,1,0:T(8,128)(2,1)}, u32[]{:S(2)}) copy-start(bf16[16,32,4096]{2,1,0:T(8,128)(2,1)} %gather_columns.3.table_ref) | copy-start | bytes 12582916
  400.7 18.9 %all-to-all-start.4 = ((bf16[16,32,512]{2,1,0:T(8,128)(2,1)}), bf16[16,32,512]{2,1,0:T(8,128)(2,1)S(1)}, u32[]{:S(2)}, u32[]{:S(2)}) async-start(bf16[16,32,512]{2,1,0:T(8,128)(2,1)} %evaluate.1), calls=%async_computation.4 | async-start | bytes 1048576 | tf_op jit(solution)/shard_map/all_to_all | solution.py:268
  419.6 60.7 %all-to-all-start.3 = ((bf16[128,4,32,128]{3,2,1,0:T(8,128)(2,1)}), bf16[128,4,32,128]{3,2,1,0:T(8,128)(2,1)}, u32[]{:S(2)}, u32[]{:S(2)}) async-start(bf16[128,4,32,128]{3,2,1,0:T(8,128)(2,1)} %scatter_columns.1), calls=%async_computation.3 | async-start | bytes 8388608 | tf_op jit(solution)/shard_map/all_to_all | solution.py:268
Sparse Core Ops, SparseCore 0:
  11.1 257.0 all-gather.1

commit v2 on v1

--- a/solution.py
+++ b/solution.py
@@ -24,6 +24,185 @@
     values = features.astype(jnp.float32)
     factor = lax.rsqrt(jnp.mean(values * values, axis=-1, keepdims=True) + 1e-05)
     return (values * factor).astype(jnp.bfloat16)
+
+
+RING = 4
+PARTS = (("x", "y", "z", 0, 1408), ("y", "z", "x", 1408, 2816), ("z", "x", "y", 2816, 4096))
+ARRIVALS = 9
+
+
+def gather_tokens_kernel(own_ref, out_ref, local_sem, send_sem, recv_sem):
+    path, shard = lax.axis_index("path"), lax.axis_index("mp")
+    me = {"z": path // RING, "y": path % RING, "x": shard // 2}
+    core = shard % 2
+
+    def shifted(axis, step):
+        return {**me, axis: (me[axis] + (step + RING)) % RING}
+
+    def device(at, which):
+        return (at["z"] * RING + at["y"], at["x"] * 2 + which)
+
+    everyone = [device(shifted(axis, step), core) for axis in "xyz" for step in (1, -1)]
+    everyone.append(device(me, 1 - core))
+    barrier = pltpu.get_barrier_semaphore()
+    for other in everyone:
+        pl.semaphore_signal(barrier, inc=1, device_id=other, device_id_type=pl.DeviceIdType.MESH)
+    pl.semaphore_wait(barrier, len(everyone))
+
+    whole = pl.ds(0, RING)
+    rows = own_ref.shape[0]
+    counter = [0]
+    sends = []
+
+    def view(at, which, lines, columns):
+        return out_ref.at[at["z"], at["y"], at["x"], which, lines, columns]
+
+    def send(at, target, lines, columns, source=None):
+        number = counter[0]
+        counter[0] += 1
+        block = view(at, core, lines, columns)
+        copy = pltpu.make_async_remote_copy(
+            src_ref=block if source is None else source,
+            dst_ref=block,
+            send_sem=send_sem.at[number],
+            recv_sem=recv_sem.at[number],
+            device_id=target,
+            device_id_type=pl.DeviceIdType.MESH,
+        )
+        copy.start()
+        sends.append(copy)
+        return number
+
+    def arrived(number, at, lines, columns, which=core):
+        block = view(at, which, lines, columns)
+        pltpu.make_async_remote_copy(
+            src_ref=block,
+            dst_ref=block,
+            send_sem=send_sem.at[number],
+            recv_sem=recv_sem.at[number],
+            device_id=device(me, 1 - core),
+            device_id_type=pl.DeviceIdType.MESH,
+        ).wait_recv()
+
+    full, low, high = pl.ds(0, rows), pl.ds(0, rows // 2), pl.ds(rows // 2, rows // 2)
+    sibling = device(me, 1 - core)
+    sibling_arrivals = []
+
+    def share(at, columns):
+        number = send(at, sibling, full, columns)
+        sibling_arrivals.append((number, at, columns))
+
+    own_copy = pltpu.make_async_copy(own_ref, view(me, core, full, pl.ds(0, own_ref.shape[1])), local_sem)
+    own_copy.start()
+
+    first = {}
+    for part, (a, b, c, begin, end) in enumerate(PARTS):
+        columns = pl.ds(begin, end - begin)
+        source = own_ref.at[:, columns]
+        first[part] = [
+            send(me, device(shifted(a, step), core), full, columns, source) for step in (1, -1)
+        ]
+    own_copy.wait()
+
+    second = {part: [] for part in range(len(PARTS))}
+
+    def send_both(at, axis, columns):
+        return [send(at, device(shifted(axis, step), core), full, columns) for step in (1, -1)]
+
+    for part, (a, b, c, begin, end) in enumerate(PARTS):
+        second[part].append(send_both(me, b, pl.ds(begin, end - begin)))
+    halves = {}
+    for index, step in ((0, 1), (1, -1)):
+        for part, (a, b, c, begin, end) in enumerate(PARTS):
+            columns = pl.ds(begin, end - begin)
+            origin = shifted(a, -step)
+            arrived(first[part][index], origin, full, columns)
+            lines = low if index == 0 else high
+            halves[part, index] = send(origin, device(shifted(a, step), core), lines, columns)
+            second[part].append(send_both(origin, b, columns))
+    for part, (a, b, c, begin, end) in enumerate(PARTS):
+        columns = pl.ds(begin, end - begin)
+        origin = shifted(a, 2)
+        arrived(halves[part, 0], origin, low, columns)
+        arrived(halves[part, 1], origin, high, columns)
+        second[part].append(send_both(origin, b, columns))
+
+    third = {part: [] for part in range(len(PARTS))}
+    for part, (a, b, c, begin, end) in enumerate(PARTS):
+        columns = pl.ds(begin, end - begin)
+        line = {**me, a: whole}
+        third[part].append(send_both(line, c, columns))
+        share(line, columns)
+
+    def origins(a):
+        return [me[a], (me[a] + 3) % RING, (me[a] + 1) % RING, (me[a] + 2) % RING]
+
+    for index, step in ((0, 1), (1, -1)):
+        lines = low if index == 0 else high
+        for part, (a, b, c, begin, end) in enumerate(PARTS):
+            columns = pl.ds(begin, end - begin)
+            far = shifted(b, -step)
+            for unit, place in enumerate(origins(a)):
+                origin = {**far, a: place}
+                arrived(second[part][unit][index], origin, full, columns)
+                halves[part, index, unit] = send(origin, device(shifted(b, step), core), lines, columns)
+            line = {**far, a: whole}
+            third[part].append(send_both(line, c, columns))
+            share(line, columns)
+    for part, (a, b, c, begin, end) in enumerate(PARTS):
+        columns = pl.ds(begin, end - begin)
+        far = shifted(b, 2)
+        for unit, place in enumerate(origins(a)):
+            origin = {**far, a: place}
+            arrived(halves[part, 0, unit], origin, low, columns)
+            arrived(halves[part, 1, unit], origin, high, columns)
+        line = {**far, a: whole}
+        third[part].append(send_both(line, c, columns))
+        share(line, columns)
+
+    for unit in range(RING):
+        for index, step in ((0, 1), (1, -1)):
+            lines = low if index == 0 else high
+            for part, (a, b, c, begin, end) in enumerate(PARTS):
+                columns = pl.ds(begin, end - begin)
+                far = {**shifted(c, -step), a: whole, b: origins(b)[unit]}
+                arrived(third[part][unit][index], far, full, columns)
+                halves[part, "last", index, unit] = send(far, device(shifted(c, step), core), lines, columns)
+                share(far, columns)
+    for unit in range(RING):
+        for part, (a, b, c, begin, end) in enumerate(PARTS):
+            columns = pl.ds(begin, end - begin)
+            far = {**shifted(c, 2), a: whole, b: origins(b)[unit]}
+            arrived(halves[part, "last", 0, unit], far, low, columns)
+            arrived(halves[part, "last", 1, unit], far, high, columns)
+            share(far, columns)
+    for number, at, columns in sibling_arrivals:
+        arrived(number, at, full, columns, 1 - core)
+    for copy in sends:
+        copy.wait_send()
+
+
+COPIES = 156
+
+
+def gather_tokens(own):
+    rows, width = own.shape
+    paths, shards = lax.axis_size("path"), lax.axis_size("mp")
+    out = pl.pallas_call(
+        gather_tokens_kernel,
+        in_specs=[pl.BlockSpec(memory_space=pl.ANY)],
+        out_specs=pl.BlockSpec(memory_space=pl.ANY),
+        out_shape=jax.ShapeDtypeStruct((paths // RING, RING, shards // 2, 2, rows, width), own.dtype),
+        scratch_shapes=[
+            pltpu.SemaphoreType.DMA,
+            pltpu.SemaphoreType.DMA((COPIES,)),
+            pltpu.SemaphoreType.DMA((COPIES,)),
+        ],
+        compiler_params=pltpu.CompilerParams(collective_id=0, has_side_effects=True),
+        cost_estimate=pl.CostEstimate(flops=0, bytes_accessed=4 * paths * shards * rows * width, transcendentals=0),
+        name="gather_tokens",
+    )(own)
+    return out.reshape(paths * shards * rows, width)
 
 
 def spread_kernel(table_ref, out_ref):
@@ -76,11 +255,13 @@
 
 def gather_kernel(blocks_ref, swap_ref, out_ref):
     quads, cols = blocks_ref.shape[0] // 4, blocks_ref.shape[2]
+    blocks = blocks_ref[:, 0].reshape(quads, 4, cols, 128)
+    line = jnp.concatenate([blocks[:, s].reshape(quads * cols, 128) for s in range(4)], axis=1)
+    turned = jnp.dot(line, swap_ref[...], preferred_element_type=jnp.float32).astype(jnp.bfloat16)
+    turned = turned.reshape(quads, cols, 512)
     for k in range(quads):
-        line = jnp.concatenate([blocks_ref[4 * k + s, 0] for s in range(4)], axis=1)
-        turned = jnp.dot(line, swap_ref[...], preferred_element_type=jnp.float32).astype(jnp.bfloat16)
         for q in range(4):
-            out_ref[q, :, k * 128 : (k + 1) * 128] = turned[:, q * 128 : (q + 1) * 128]
+            out_ref[q, :, k * 128 : (k + 1) * 128] = turned[k, :, q * 128 : (q + 1) * 128]
 
 
 def gather_columns(blocks):
@@ -99,30 +280,61 @@
     )(blocks, swap_matrix())
 
 
-def scatter_kernel(table_ref, swap_ref, out_ref):
-    quads = out_ref.shape[0] // 4
-    for k in range(quads):
-        line = jnp.concatenate([table_ref[q, :, k * 128 : (k + 1) * 128] for q in range(4)], axis=1)
+CHUNK = 8
+
+
+def outer_kernel(counts_ref, sums_ref, table_ref, speed_ref, swap_ref, updated_ref, out_ref):
+    group = pl.program_id(0)
+    quads, cols = out_ref.shape[0] // 4, out_ref.shape[2]
+    counts = [counts_ref[4 * group + q] for q in range(4)]
+    for begin in range(0, quads, CHUNK):
+        blocks = speed_ref[4 * begin : 4 * (begin + CHUNK), 0].reshape(CHUNK, 4, cols, 128)
+        line = jnp.concatenate([blocks[:, s].reshape(CHUNK * cols, 128) for s in range(4)], axis=1)
+        speed = jnp.dot(line, swap_ref[...], preferred_element_type=jnp.float32).reshape(CHUNK, cols, 512)
+        lines = []
+        for k in range(CHUNK):
+            pieces_of = []
+            for q in range(4):
+                columns = slice((begin + k) * 128, (begin + k + 1) * 128)
+                average = sums_ref[q, :, columns] / counts[q]
+                moment = outer_momentum * speed[k, :, q * 128 : (q + 1) * 128] + average
+                begun = table_ref[q, :, columns].astype(jnp.float32)
+                updated_ref[q, :, columns] = (
+                    begun - outer_rate * (average + outer_momentum * moment)
+                ).astype(jnp.bfloat16)
+                pieces_of.append(moment.astype(jnp.bfloat16))
+            lines.append(jnp.concatenate(pieces_of, axis=1))
+        line = jnp.concatenate(lines, axis=0)
         turned = jnp.dot(line, swap_ref[...], preferred_element_type=jnp.float32).astype(jnp.bfloat16)
-        for s in range(4):
-            out_ref[4 * k + s, 0] = turned[:, s * 128 : (s + 1) * 128]
-
-
-def scatter_columns(table):
+        turned = turned.reshape(CHUNK, cols, 512)
+        for k in range(CHUNK):
+            for s in range(4):
+                out_ref[4 * (begin + k) + s, 0] = turned[k, :, s * 128 : (s + 1) * 128]
+
+
+def outer_step(counts, sums, table, speed):
     modules, cols, width = table.shape
-    groups, devices = modules // 4, width // 32
+    devices, groups = speed.shape[:2]
+    rows = pl.BlockSpec((4, cols, width), lambda g: (g, 0, 0))
+    blocks = pl.BlockSpec((devices, 1, cols, 128), lambda g: (0, g, 0, 0))
     return pl.pallas_call(
-        scatter_kernel,
+        outer_kernel,
         grid=(groups,),
         in_specs=[
-            pl.BlockSpec((4, cols, width), lambda g: (g, 0, 0)),
+            pl.BlockSpec(memory_space=pltpu.SMEM),
+            rows,
+            rows,
+            blocks,
             pl.BlockSpec((512, 512), lambda g: (0, 0)),
         ],
-        out_specs=pl.BlockSpec((devices, 1, cols, 128), lambda g: (0, g, 0, 0)),
-        out_shape=jax.ShapeDtypeStruct((devices, groups, cols, 128), table.dtype),
+        out_specs=[rows, blocks],
+        out_shape=[
+            jax.ShapeDtypeStruct(table.shape, table.dtype),
+            jax.ShapeDtypeStruct(speed.shape, speed.dtype),
+        ],
         compiler_params=pltpu.CompilerParams(vmem_limit_bytes=VMEM_LIMIT),
-        name="scatter_columns",
-    )(table, swap_matrix())
+        name="outer_step",
+    )(counts, sums, table, speed, swap_matrix())
 
 
 def pieces(value):
@@ -135,7 +347,7 @@
 
 def slopes(weights, normed, goal):
     cols = goal.shape[0]
-    both = lax.dot_general(weights, normed, NT, preferred_element_type=jnp.float32)
+    both = jnp.dot(weights, normed, preferred_element_type=jnp.float32)
     gate_act, up_act = both[:cols], both[cols:]
     sigma = jax.nn.sigmoid(gate_act)
     swish = gate_act * sigma
@@ -148,7 +360,7 @@
 TILE = 512
 
 
-def inner_kernel(lists_ref, normed_ref, goal_ref, table_ref, sums_ref, start, current, first_grad, slope):
+def inner_kernel(lists_ref, normed_ref, goal_ref, table_ref, sums_ref, start, current, first_grad, slope, turned):
     path = pl.program_id(0)
     gate, up = lists_ref[2 * path], lists_ref[2 * path + 1]
     cols = goal_ref.shape[1]
@@ -161,7 +373,9 @@
     start[:cols] = table_ref[gate]
     start[cols:] = table_ref[up]
     goal = goal_ref[0].astype(jnp.float32)
-    slope[...] = slopes(start[...], normed_ref[...], goal)
+    for j in range(width // TILE):
+        turned[j * TILE : (j + 1) * TILE, :] = normed_ref[:, j * TILE : (j + 1) * TILE].T
+    slope[...] = slopes(start[...], turned[...], goal)
 
     def product(columns):
         parts = jnp.dot(slope[...], normed_ref[:, columns], preferred_element_type=jnp.float32)
@@ -177,7 +391,7 @@
         begin = start[:, columns].astype(jnp.float32)
         current[:, columns] = after_first(begin, grad).astype(jnp.bfloat16)
 
-    slope[...] = slopes(current[...], normed_ref[...], goal)
+    slope[...] = slopes(current[...], turned[...], goal)
     for j in range(width // TILE):
         columns = slice(j * TILE, (j + 1) * TILE)
         grad = product(columns)
@@ -218,6 +432,7 @@
                 pltpu.VMEM((2 * cols, width), jnp.bfloat16),
                 pltpu.VMEM((2 * cols, width), jnp.float32),
                 pltpu.VMEM((6 * cols, TOK_PATH), jnp.bfloat16),
+                pltpu.VMEM((width, TOK_PATH), jnp.bfloat16),
             ],
         ),
         out_shape=jax.ShapeDtypeStruct((modules, cols, width), jnp.float32),
@@ -276,28 +491,20 @@
     lists = path_lists.reshape(-1)
     both = ("path", "mp")
 
-    def to_columns(table):
+    def sent(table):
         blocks = spread(table, paths, shards)
-        blocks = blocks.reshape((paths * shards,) + blocks.shape[2:])
-        return gather_columns(exchange(blocks, both))
-
-    def to_rows(table):
-        blocks = exchange(scatter_columns(table), both)
-        return unspread(blocks.reshape((paths, shards) + blocks.shape[1:]), modules, rows_own)
-
-    normed = lax.all_gather(normalize(features), both, axis=0, tiled=True)
-    table = to_columns(module_table)
+        return exchange(blocks.reshape((paths * shards,) + blocks.shape[2:]), both)
+
+    normed = gather_tokens(normalize(features))
+    table = gather_columns(sent(module_table))
     goals = exchange(targets.T.reshape(paths, cols, TOK_PATH), "path")
-    speed = to_columns(momentum)
-    sums = inner_steps(lists, normed, goals, table)
+    speed = sent(momentum)
     select = lists[None, :] == jnp.arange(modules, dtype=jnp.int32)[:, None]
     counts = jnp.sum(select.astype(jnp.float32), axis=1)
-    average = sums / counts[:, None, None]
-    moment = outer_momentum * speed.astype(jnp.float32) + average
-    updated = (
-        table.astype(jnp.float32) - outer_rate * (average + outer_momentum * moment)
-    ).astype(jnp.bfloat16)
-    momentum_out = to_rows(moment.astype(jnp.bfloat16))
+    sums = inner_steps(lists, normed, goals, table)
+    updated, blocks = lax.optimization_barrier(outer_step(counts, sums, table, speed))
+    blocks = exchange(blocks, both)
+    momentum_out = unspread(blocks.reshape((paths, shards) + blocks.shape[1:]), modules, rows_own)
     evaluated = evaluate(lists, normed, updated)
     evaluated = exchange(evaluated, "path").reshape(paths * cols, TOK_PATH).T
     return (momentum_out, evaluated)

time: 496 us -> 488 us (0.984)
  Pallas kernels: 190 us -> 334 us
  waiting for transfers between devices: 241 us -> 100 us
  blocking collectives: 0 us -> 17.8 us
  between operations: 14.1 us -> 0.72 us
  other arithmetic: 12.5 us -> 2.75 us
  starting transfers between devices: 34 us -> 27.4 us
    pallas_call x1 -> x2, Pallas kernels: 14.3 us -> 192 us  [the longest x1 180 us: gather_tokens(): pl.pallas_call(gather_tokens_kernel, in_specs=[pl.BlockSpec(memory_space=...]
    all_gather x1 -> x0, waiting for transfers between devices: 72.2 us -> none  [local(): normed = lax.all_gather(normalize(features), both, axis=0, tiled=True)]
    all_to_all x5 -> x4, waiting for transfers between devices: 169 us -> 100 us  [exchange(): return lax.all_to_all(blocks, axes, split_axis=0, concat_axis=0, tiled=True)]
    pallas_call x2 -> x1, Pallas kernels: 30.2 us -> 6.21 us  [gather_columns(): pl.pallas_call(gather_kernel, grid=(groups,), in_specs=[pl.BlockSpec((dev...]
    all_to_all x0 -> x1, blocking collectives: none -> 17.8 us  [exchange(): return lax.all_to_all(blocks, axes, split_axis=0, concat_axis=0, tiled=True)]
    pallas_call x1, Pallas kernels: 90.6 us -> 80 us  [inner_steps(): pl.pallas_call(inner_kernel, grid_spec=pltpu.PrefetchScalarGridSpec(num_s...]
    convert_element_type x1 -> x0, other arithmetic: 8.18 us -> none  [local(): updated = (table.astype(jnp.float32) - outer_rate * (average + outer_mome...]
    all_to_all x5 -> x4, starting transfers between devices: 33.9 us -> 27.4 us  [exchange(): return lax.all_to_all(blocks, axes, split_axis=0, concat_axis=0, tiled=True)]
  transfers between devices with their start and end apart: 6 -> 4, of which waited for: 4 -> 3; matrix products, arithmetic and copies ran while one was open for 1% -> 1% of each run, Pallas kernels for 12% -> 58%
where the time goes in v2:
time: 488 us; the launch traced here: 486 us
  Pallas kernels  334 us (68%)
  waiting for transfers between devices  100 us (20%)
  starting transfers between devices  27.4 us (6%)
  blocking collectives  17.8 us (4%)
    pallas_call x1, Pallas kernels, gather_tokens(): pl.pallas_call(gather_tokens_kernel, in_specs=[pl.BlockSpec(memory_space=...  180 us
    all_to_all x4, waiting for transfers between devices, exchange(): return lax.all_to_all(blocks, axes, split_axis=0, concat_axis=0, tiled=True)  100 us
    pallas_call x1, Pallas kernels, inner_steps(): pl.pallas_call(inner_kernel, grid_spec=pltpu.PrefetchScalarGridSpec(num_s...  80 us
    pallas_call x1, Pallas kernels, evaluate(): pl.pallas_call(evaluate_kernel, grid_spec=pltpu.PrefetchScalarGridSpec(nu...  33.7 us
    all_to_all x4, starting transfers between devices, exchange(): return lax.all_to_all(blocks, axes, split_axis=0, concat_axis=0, tiled=True)  27.4 us
    all_to_all x1, blocking collectives, exchange(): return lax.all_to_all(blocks, axes, split_axis=0, concat_axis=0, tiled=True)  17.8 us
    pallas_call x2, Pallas kernels, spread(): pl.pallas_call(spread_kernel, grid=(shards,), in_specs=[pl.BlockSpec((gro...  14.4 us
    pallas_call x1, Pallas kernels, outer_step(): pl.pallas_call(outer_kernel, grid=(groups,), in_specs=[pl.BlockSpec(memor...  12.2 us
  transfers between devices with their start and end apart: 4, of which 3 were waited for; matrix products, arithmetic and copies ran while one was open for 1% of the time, Pallas kernels for 58%

profile of v2, /device:TPU:1, one launch (start us, length us, event | category | flops | bytes accessed | tf_op | source)
XLA Modules:
  0.0 486.5 jit_solution(14858096904914782495)
XLA Ops:
  0.6 2.0 copy.14
  2.7 8.6 %all-to-all-start = ((bf16[16,32,512]{2,1,0:T(8,128)(2,1)}), bf16[16,32,512]{2,1,0:T(8,128)(2,1)S(1)}, u32[]{:S(2)}, u32[]{:S(2)}) async-start(bf16[16,32,512]{2,1,0:T(8,128)(2,1)} %bitcast.2), calls=%async_computation | async-start | bytes 1048576 | tf_op jit(solution)/shard_map/all_to_all | solution.py:483
  11.3 7.2 %spread.2 = bf16[16,8,4,32,128]{4,3,2,1,0:T(8,128)(2,1)} custom-call(bf16[4,128,4096]{2,1,0:T(8,128)(2,1)} %bitcast.13), custom_call_target="tpu_custom_call" | custom-call | tf_op jit(solution)/shard_map/spread/pallas_call | solution.py:219
  18.5 3.3 all-to-all-done.goal_ref
  21.8 0.0 copy-start.1
  21.8 0.0 copy-start.3
  21.8 0.8 copy-done.1
  22.6 7.5 %all-to-all-start.1 = ((bf16[128,4,32,128]{3,2,1,0:T(8,128)(2,1)}), bf16[128,4,32,128]{3,2,1,0:T(8,128)(2,1)}, u32[]{:S(2)}, u32[]{:S(2)}) async-start(bf16[128,4,32,128]{3,2,1,0:T(8,128)(2,1)} %bitcast.12), calls=%async_computation.1 | async-start | bytes 8388608 | tf_op jit(solution)/shard_map/all_to_all | solution.py:483
  30.1 0.0 copy-done.3
  30.1 0.1 copy.13
  30.2 0.1 eq.46.lists_ref
  30.3 0.0 copy-start.2
  30.3 0.0 copy-start
  30.3 7.3 %spread.3 = bf16[16,8,4,32,128]{4,3,2,1,0:T(8,128)(2,1)} custom-call(bf16[4,128,4096]{2,1,0:T(8,128)(2,1)} %bitcast.14), custom_call_target="tpu_custom_call" | custom-call | tf_op jit(solution)/shard_map/spread/pallas_call | solution.py:219
  37.6 0.0 copy-done
  37.6 0.2 fusion
  37.8 45.0 %all-to-all-done.1.blocks_ref = bf16[128,4,32,128]{3,2,1,0:T(8,128)(2,1)} async-done(((bf16[128,4,32,128]{3,2,1,0:T(8,128)(2,1)}), bf16[128,4,32,128]{3,2,1,0:T(8,128)(2,1)}, u32[]{:S(2)}, u32[]{:S(2)}) %all-to-all-start.1) | async-done | bytes 4194336 | tf_op jit(solution)/shard_map/all_to_all | solution.py:483
  82.8 5.5 %all-to-all-start.2 = ((bf16[128,4,32,128]{3,2,1,0:T(8,128)(2,1)}), bf16[128,4,32,128]{3,2,1,0:T(8,128)(2,1)}, u32[]{:S(2)}, u32[]{:S(2)}) async-start(bf16[128,4,32,128]{3,2,1,0:T(8,128)(2,1)} %bitcast.11), calls=%async_computation.2 | async-start | bytes 8388608 | tf_op jit(solution)/shard_map/all_to_all | solution.py:483
  88.3 0.9 fusion.1.own_ref
  89.2 180.1 %gather_tokens.1 = bf16[4,4,4,2,64,4096]{5,4,3,2,1,0:T(8,128)(2,1)} custom-call(bf16[64,4096]{1,0:T(8,128)(2,1)} %fusion.1.own_ref), custom_call_target="tpu_custom_call" | custom-call | bytes 134217728 | tf_op jit(solution)/shard_map/gather_tokens/pallas_call | solution.py:191
  269.3 0.0 copy-done.2
  269.3 0.6 convert_reduce_fusion.counts_ref
  269.9 0.9 fusion.2.swap_ref
  270.9 6.2 %gather_columns.1.table_ref = bf16[16,32,4096]{2,1,0:T(8,128)(2,1)} custom-call(bf16[128,4,32,128]{3,2,1,0:T(8,128)(2,1)} %all-to-all-done.1.blocks_ref, bf16[512,512]{1,0:T(8,128)(2,1)} %fusion.2.swap_ref), custom_call_target="tpu_custom_call" | custom-call | tf_op jit(solution)/shard_map/gather_columns/pallas_call | solution.py:269
  277.1 80.0 %inner_steps.1.sums_ref = f32[16,32,4096]{2,1,0:T(8,128)} custom-call(s32[32]{0:T(128)} %copy-done.2, bf16[8192,4096]{1,0:T(8,128)(2,1)} %bitcast.normed_ref, bf16[16,32,512]{2,1,0:T(8,128)(2,1)} %copy-done.1, bf16[16,32,4096]{2,1,0:T(8,128)(2,1)} %gather_columns.1.table_ref), custom_call_target="tpu_custom_call" | custom-call | flops 34359738368 | bytes 67108864 | tf_op jit(solution)/shard_map/inner_steps/pallas_call | solution.py:419
  357.0 0.0 all-to-all-done.2.speed_ref
  357.0 12.2 %outer_step.1 = (bf16[16,32,4096]{2,1,0:T(8,128)(2,1)}, bf16[128,4,32,128]{3,2,1,0:T(8,128)(2,1)}) custom-call(f32[16]{0:T(128)} %convert_reduce_fusion.counts_ref, f32[16,32,4096]{2,1,0:T(8,128)} %inner_steps.1.sums_ref, bf16[16,32,4096]{2,1,0:T(8,128)(2,1)} %gather_columns.1.table_ref, bf16[128,4,32,128]{3,2,1,0:T(8,128)(2,1)} %all-to-all-done.2.speed_ref, ...), custom_call_target="tpu_custom_call" | custom-call | tf_op jit(solution)/shard_map/outer_step/pallas_call | solution.py:320
  369.2 33.7 %evaluate.1 = bf16[16,32,512]{2,1,0:T(8,128)(2,1)} custom-call(s32[32]{0:T(128)} %copy-done.2, bf16[8192,4096]{1,0:T(8,128)(2,1)} %bitcast.normed_ref, bf16[16,32,4096]{2,1,0:T(8,128)(2,1)} %get-tuple-element.5.table_ref), custom_call_target="tpu_custom_call" | custom-call | flops 4294967296 | bytes 67108864 | tf_op jit(solution)/shard_map/evaluate/pallas_call | solution.py:461
  402.9 17.8 %all_to_all.25 = bf16[16,32,512]{2,1,0:T(8,128)(2,1)S(1)} all-to-all(bf16[16,32,512]{2,1,0:T(8,128)(2,1)} %evaluate.1), channel_id=1, replica_groups=mesh['path'=16,'mp'=8] {'path'}, dimensions={0} | all-to-all | bytes 1048576 | tf_op jit(solution)/shard_map/all_to_all | solution.py:483
  420.7 5.8 %all-to-all-start.3 = ((bf16[128,4,32,128]{3,2,1,0:T(8,128)(2,1)}), bf16[128,4,32,128]{3,2,1,0:T(8,128)(2,1)}, u32[]{:S(2)}, u32[]{:S(2)}) async-start(bf16[128,4,32,128]{3,2,1,0:T(8,128)(2,1)} %get-tuple-element.4), calls=%async_computation.3 | async-start | bytes 8388608 | tf_op jit(solution)/shard_map/all_to_all | solution.py:483
  426.5 1.0 copy.15
  427.5 51.8 %all-to-all-done.3 = bf16[128,4,32,128]{3,2,1,0:T(8,128)(2,1)} async-done(((bf16[128,4,32,128]{3,2,1,0:T(8,128)(2,1)}), bf16[128,4,32,128]{3,2,1,0:T(8,128)(2,1)}, u32[]{:S(2)}, u32[]{:S(2)}) %all-to-all-start.3) | async-done | bytes 4194336 | tf_op jit(solution)/shard_map/all_to_all | solution.py:483
  479.3 7.2 %unspread.1 = bf16[4,128,4096]{2,1,0:T(8,128)(2,1)} custom-call(bf16[16,8,4,32,128]{4,3,2,1,0:T(8,128)(2,1)} %bitcast.7.blocks_ref), custom_call_target="tpu_custom_call" | custom-call | tf_op jit(solution)/shard_map/unspread/pallas_call | solution.py:238
  (2 shorter events, 0.0 us)
Async XLA Ops:
  2.7 19.1 %all-to-all-start = ((bf16[16,32,512]{2,1,0:T(8,128)(2,1)}), bf16[16,32,512]{2,1,0:T(8,128)(2,1)S(1)}, u32[]{:S(2)}, u32[]{:S(2)}) async-start(bf16[16,32,512]{2,1,0:T(8,128)(2,1)} %bitcast.2), calls=%async_computation | async-start | bytes 1048576 | tf_op jit(solution)/shard_map/all_to_all | solution.py:483
  21.8 0.8 copy-start.1
  21.8 8.3 %copy-start.3 = (s32[16,2]{0,1:T(2,128)S(1)}, s32[16,2]{0,1:T(2,128)}, u32[]{:S(2)}) copy-start(s32[16,2]{0,1:T(2,128)} %param.9) | copy-start | bytes 388
  22.6 60.2 %all-to-all-start.1 = ((bf16[128,4,32,128]{3,2,1,0:T(8,128)(2,1)}), bf16[128,4,32,128]{3,2,1,0:T(8,128)(2,1)}, u32[]{:S(2)}, u32[]{:S(2)}) async-start(bf16[128,4,32,128]{3,2,1,0:T(8,128)(2,1)} %bitcast.12), calls=%async_computation.1 | async-start | bytes 8388608 | tf_op jit(solution)/shard_map/all_to_all | solution.py:483
  30.3 239.0 %copy-start.2 = (s32[32]{0:T(128)}, s32[32]{0:T(128)S(1)}, u32[]{:S(2)}) copy-start(s32[32]{0:T(128)S(1)} %eq.46.lists_ref) | copy-start | bytes 388
  30.3 7.3 %copy-start = (bf16[64,4096]{1,0:T(8,128)(2,1)S(1)}, bf16[64,4096]{1,0:T(8,128)(2,1)}, u32[]{:S(2)}) copy-start(bf16[64,4096]{1,0:T(8,128)(2,1)} %param.5) | copy-start | bytes 1572868
  82.8 274.3 %all-to-all-start.2 = ((bf16[128,4,32,128]{3,2,1,0:T(8,128)(2,1)}), bf16[128,4,32,128]{3,2,1,0:T(8,128)(2,1)}, u32[]{:S(2)}, u32[]{:S(2)}) async-start(bf16[128,4,32,128]{3,2,1,0:T(8,128)(2,1)} %bitcast.11), calls=%async_computation.2 | async-start | bytes 8388608 | tf_op jit(solution)/shard_map/all_to_all | solution.py:483
  420.7 58.6 %all-to-all-start.3 = ((bf16[128,4,32,128]{3,2,1,0:T(8,128)(2,1)}), bf16[128,4,32,128]{3,2,1,0:T(8,128)(2,1)}, u32[]{:S(2)}, u32[]{:S(2)}) async-start(bf16[128,4,32,128]{3,2,1,0:T(8,128)(2,1)} %get-tuple-element.4), calls=%async_computation.3 | async-start | bytes 8388608 | tf_op jit(solution)/shard_map/all_to_all | solution.py:483

commit v3 on v2

--- a/solution.py
+++ b/solution.py
@@ -31,7 +31,7 @@
 ARRIVALS = 9
 
 
-def gather_tokens_kernel(own_ref, out_ref, local_sem, send_sem, recv_sem):
+def gather_tokens_kernel(own_ref, goal_ref, out_ref, goals_ref, local_sem, send_sem, recv_sem, goal_sem, goals_sem):
     path, shard = lax.axis_index("path"), lax.axis_index("mp")
     me = {"z": path // RING, "y": path % RING, "x": shard // 2}
     core = shard % 2
@@ -44,6 +44,9 @@
 
     everyone = [device(shifted(axis, step), core) for axis in "xyz" for step in (1, -1)]
     everyone.append(device(me, 1 - core))
+    paths = goal_ref.shape[0]
+    peers = [((path + step) % paths, shard) for step in range(1, paths)]
+    everyone += peers
     barrier = pltpu.get_barrier_semaphore()
     for other in everyone:
         pl.semaphore_signal(barrier, inc=1, device_id=other, device_id_type=pl.DeviceIdType.MESH)
@@ -103,6 +106,21 @@
             send(me, device(shifted(a, step), core), full, columns, source) for step in (1, -1)
         ]
     own_copy.wait()
+
+    own_goal = pltpu.make_async_copy(goal_ref.at[path], goals_ref.at[path], goals_sem.at[0])
+    own_goal.start()
+    goal_copies = []
+    for step, other in enumerate(peers, 1):
+        copy = pltpu.make_async_remote_copy(
+            src_ref=goal_ref.at[other[0]],
+            dst_ref=goals_ref.at[path],
+            send_sem=goal_sem.at[step],
+            recv_sem=goals_sem.at[step],
+            device_id=other,
+            device_id_type=pl.DeviceIdType.MESH,
+        )
+        copy.start()
+        goal_copies.append(copy)
 
     second = {part: [] for part in range(len(PARTS))}
 
@@ -178,6 +196,18 @@
             share(far, columns)
     for number, at, columns in sibling_arrivals:
         arrived(number, at, full, columns, 1 - core)
+    own_goal.wait()
+    for step, copy in enumerate(goal_copies, 1):
+        copy.wait_send()
+        block = goals_ref.at[(path + paths - step) % paths]
+        pltpu.make_async_remote_copy(
+            src_ref=block,
+            dst_ref=block,
+            send_sem=goal_sem.at[step],
+            recv_sem=goals_sem.at[step],
+            device_id=peers[0],
+            device_id_type=pl.DeviceIdType.MESH,
+        ).wait_recv()
     for copy in sends:
         copy.wait_send()
 
@@ -185,24 +215,32 @@
 COPIES = 156
 
 
-def gather_tokens(own):
+def gather_tokens(own, goal):
     rows, width = own.shape
     paths, shards = lax.axis_size("path"), lax.axis_size("mp")
-    out = pl.pallas_call(
+    anywhere = pl.BlockSpec(memory_space=pl.ANY)
+    out, goals = pl.pallas_call(
         gather_tokens_kernel,
-        in_specs=[pl.BlockSpec(memory_space=pl.ANY)],
-        out_specs=pl.BlockSpec(memory_space=pl.ANY),
-        out_shape=jax.ShapeDtypeStruct((paths // RING, RING, shards // 2, 2, rows, width), own.dtype),
+        in_specs=[anywhere, anywhere],
+        out_specs=[anywhere, anywhere],
+        out_shape=[
+            jax.ShapeDtypeStruct((paths // RING, RING, shards // 2, 2, rows, width), own.dtype),
+            jax.ShapeDtypeStruct(goal.shape, goal.dtype),
+        ],
         scratch_shapes=[
             pltpu.SemaphoreType.DMA,
             pltpu.SemaphoreType.DMA((COPIES,)),
             pltpu.SemaphoreType.DMA((COPIES,)),
+            pltpu.SemaphoreType.DMA((paths,)),
+            pltpu.SemaphoreType.DMA((paths,)),
         ],
         compiler_params=pltpu.CompilerParams(collective_id=0, has_side_effects=True),
-        cost_estimate=pl.CostEstimate(flops=0, bytes_accessed=4 * paths * shards * rows * width, transcendentals=0),
+        cost_estimate=pl.CostEstimate(
+            flops=0, bytes_accessed=4 * paths * shards * rows * width, transcendentals=0
+        ),
         name="gather_tokens",
-    )(own)
-    return out.reshape(paths * shards * rows, width)
+    )(own, goal)
+    return out.reshape(paths * shards * rows, width), goals
 
 
 def spread_kernel(table_ref, out_ref):
@@ -444,14 +482,54 @@
     )(lists, normed, goals, table)
 
 
-def evaluate_kernel(lists_ref, normed_ref, table_ref, out_ref, weights):
-    path = pl.program_id(0)
-    cols = out_ref.shape[1]
-    weights[:cols] = table_ref[lists_ref[2 * path]]
-    weights[cols:] = table_ref[lists_ref[2 * path + 1]]
+def evaluate_kernel(lists_ref, normed_ref, table_ref, out_ref, weights, outgoing, arrived, send_sem, recv_sem):
+    target = pl.program_id(0)
+    path, shard = lax.axis_index("path"), lax.axis_index("mp")
+    paths, cols, tokens = arrived.shape
+
+    def remote(block, at, number, other):
+        return pltpu.make_async_remote_copy(
+            src_ref=outgoing.at[block],
+            dst_ref=arrived.at[at],
+            send_sem=send_sem.at[block],
+            recv_sem=recv_sem.at[number],
+            device_id=(other, shard),
+            device_id_type=pl.DeviceIdType.MESH,
+        )
+
+    @pl.when(target == 0)
+    def _():
+        barrier = pltpu.get_barrier_semaphore()
+        for step in range(1, paths):
+            pl.semaphore_signal(
+                barrier,
+                inc=1,
+                device_id=((path + step) % paths, shard),
+                device_id_type=pl.DeviceIdType.MESH,
+            )
+        pl.semaphore_wait(barrier, paths - 1)
+
+    weights[:cols] = table_ref[lists_ref[2 * target]]
+    weights[cols:] = table_ref[lists_ref[2 * target + 1]]
     both = lax.dot_general(weights[...], normed_ref[...], NT, preferred_element_type=jnp.float32)
     gate_act = both[:cols]
-    out_ref[0] = (gate_act * jax.nn.sigmoid(gate_act) * both[cols:]).astype(jnp.bfloat16)
+    result = (gate_act * jax.nn.sigmoid(gate_act) * both[cols:]).astype(jnp.bfloat16)
+
+    @pl.when(target == path)
+    def _():
+        arrived[path] = result
+
+    @pl.when(target != path)
+    def _():
+        outgoing[target] = result
+        remote(target, path, path, target).start()
+
+    @pl.when(target == paths - 1)
+    def _():
+        for step in range(1, paths):
+            other = (path + step) % paths
+            remote(other, other, other, other).wait()
+        out_ref[...] = arrived[...].reshape(paths * cols, tokens).T
 
 
 def evaluate(lists, normed, table):
@@ -460,18 +538,24 @@
     paths = tokens // TOK_PATH
     return pl.pallas_call(
         evaluate_kernel,
-        grid_spec=pltpu.PrefetchScalarGridSpec(
-            num_scalar_prefetch=1,
-            grid=(paths,),
-            in_specs=[
-                pl.BlockSpec((TOK_PATH, width), lambda p, s: (p, 0)),
-                pl.BlockSpec((modules, cols, width), lambda p, s: (0, 0, 0)),
-            ],
-            out_specs=pl.BlockSpec((1, cols, TOK_PATH), lambda p, s: (p, 0, 0)),
-            scratch_shapes=[pltpu.VMEM((2 * cols, width), jnp.bfloat16)],
+        grid=(paths,),
+        in_specs=[
+            pl.BlockSpec(memory_space=pltpu.SMEM),
+            pl.BlockSpec((TOK_PATH, width), lambda p: (p, 0)),
+            pl.BlockSpec((modules, cols, width), lambda p: (0, 0, 0)),
+        ],
+        out_specs=pl.BlockSpec((TOK_PATH, paths * cols), lambda p: (0, 0)),
+        scratch_shapes=[
+            pltpu.VMEM((2 * cols, width), jnp.bfloat16),
+            pltpu.VMEM((paths, cols, TOK_PATH), jnp.bfloat16),
+            pltpu.VMEM((paths, cols, TOK_PATH), jnp.bfloat16),
+            pltpu.SemaphoreType.DMA((paths,)),
+            pltpu.SemaphoreType.DMA((paths,)),
+        ],
+        out_shape=jax.ShapeDtypeStruct((TOK_PATH, paths * cols), jnp.bfloat16),
+        compiler_params=pltpu.CompilerParams(
+            vmem_limit_bytes=VMEM_LIMIT, collective_id=1, has_side_effects=True
         ),
-        out_shape=jax.ShapeDtypeStruct((paths, cols, TOK_PATH), jnp.bfloat16),
-        compiler_params=pltpu.CompilerParams(vmem_limit_bytes=VMEM_LIMIT),
         cost_estimate=pl.CostEstimate(
             flops=4 * tokens * width * cols, bytes_accessed=2 * tokens * width, transcendentals=0
         ),
@@ -491,22 +575,25 @@
     lists = path_lists.reshape(-1)
     both = ("path", "mp")
 
-    def sent(table):
-        blocks = spread(table, paths, shards)
-        return exchange(blocks.reshape((paths * shards,) + blocks.shape[2:]), both)
-
-    normed = gather_tokens(normalize(features))
-    table = gather_columns(sent(module_table))
-    goals = exchange(targets.T.reshape(paths, cols, TOK_PATH), "path")
-    speed = sent(momentum)
+    def sent(blocks):
+        return exchange(blocks.reshape((paths * shards,) + blocks.shape[-3:]), both)
+
+    own, goal = normalize(features), targets.T.reshape(paths, cols, TOK_PATH)
+    speed, module_table, own, goal = lax.optimization_barrier(
+        (spread(momentum, paths, shards), spread(module_table, paths, shards), own, goal)
+    )
+    arrived = sent(module_table)
+    normed, goals = gather_tokens(own, goal)
+    arrived, normed, speed = lax.optimization_barrier((arrived, normed, speed))
+    speed = sent(speed)
+    table = gather_columns(arrived)
     select = lists[None, :] == jnp.arange(modules, dtype=jnp.int32)[:, None]
     counts = jnp.sum(select.astype(jnp.float32), axis=1)
     sums = inner_steps(lists, normed, goals, table)
     updated, blocks = lax.optimization_barrier(outer_step(counts, sums, table, speed))
-    blocks = exchange(blocks, both)
+    blocks = sent(blocks)
+    evaluated = evaluate(lists, normed, updated)
     momentum_out = unspread(blocks.reshape((paths, shards) + blocks.shape[1:]), modules, rows_own)
-    evaluated = evaluate(lists, normed, updated)
-    evaluated = exchange(evaluated, "path").reshape(paths * cols, TOK_PATH).T
     return (momentum_out, evaluated)
 
 

time: 488 us -> 403 us (0.83)
  waiting for transfers between devices: 100 us -> 2.73 us
  Pallas kernels: 334 us -> 357 us
  blocking collectives: 17.8 us -> 0 us
    all_to_all x4 -> x3, waiting for transfers between devices: 100 us -> 2.73 us  [exchange(): return lax.all_to_all(blocks, axes, split_axis=0, concat_axis=0, tiled=True)]
    pallas_call x2, Pallas kernels: 214 us -> 237 us  [the longest x1 187 us: gather_tokens(): pl.pallas_call(gather_tokens_kernel, in_specs=[anywhere, anywhere], out_s...]
    all_to_all x1 -> x0, blocking collectives: 17.8 us -> none  [exchange(): return lax.all_to_all(blocks, axes, split_axis=0, concat_axis=0, tiled=True)]
    all_to_all x4 -> x3, starting transfers between devices: 27.4 us -> 30 us  [exchange(): return lax.all_to_all(blocks, axes, split_axis=0, concat_axis=0, tiled=True)]
  transfers between devices with their start and end apart: 4 -> 3, of which waited for: 3 -> 1; matrix products, arithmetic and copies ran while one was open for 1% -> 0% of each run, Pallas kernels for 58% -> 81%
where the time goes in v3:
time: 403 us; the launch traced here: 398 us
  Pallas kernels  357 us (89%)
  starting transfers between devices  30 us (7%)
  other arithmetic  4.84 us (1%)
    pallas_call x1, Pallas kernels, gather_tokens(): pl.pallas_call(gather_tokens_kernel, in_specs=[anywhere, anywhere], out_s...  187 us
    pallas_call x1, Pallas kernels, inner_steps(): pl.pallas_call(inner_kernel, grid_spec=pltpu.PrefetchScalarGridSpec(num_s...  80 us
    pallas_call x1, Pallas kernels, evaluate(): pl.pallas_call(evaluate_kernel, grid=(paths,), in_specs=[pl.BlockSpec(mem...  50.4 us
    all_to_all x3, starting transfers between devices, exchange(): return lax.all_to_all(blocks, axes, split_axis=0, concat_axis=0, tiled=True)  30 us
    pallas_call x2, Pallas kernels, spread(): pl.pallas_call(spread_kernel, grid=(shards,), in_specs=[pl.BlockSpec((gro...  14.4 us
    pallas_call x1, Pallas kernels, outer_step(): pl.pallas_call(outer_kernel, grid=(groups,), in_specs=[pl.BlockSpec(memor...  12.1 us
  transfers between devices with their start and end apart: 3, of which 1 were waited for; matrix products, arithmetic and copies ran while one was open for 0% of the time, Pallas kernels for 81%

profile of v3, /device:TPU:1, one launch (start us, length us, event | category | flops | bytes accessed | tf_op | source)
XLA Modules:
  0.0 398.5 jit_solution(17938251541805600645)
XLA Ops:
  0.6 1.2 fusion
  1.9 2.0 fusion.1.own_ref
  3.9 2.0 copy.12
  5.9 7.2 %spread.3 = bf16[16,8,4,32,128]{4,3,2,1,0:T(8,128)(2,1)} custom-call(bf16[4,128,4096]{2,1,0:T(8,128)(2,1)} %bitcast.11), custom_call_target="tpu_custom_call" | custom-call | tf_op jit(solution)/shard_map/spread/pallas_call | solution.py:257
  13.1 7.2 %spread.2 = bf16[16,8,4,32,128]{4,3,2,1,0:T(8,128)(2,1)} custom-call(bf16[4,128,4096]{2,1,0:T(8,128)(2,1)} %bitcast.12), custom_call_target="tpu_custom_call" | custom-call | tf_op jit(solution)/shard_map/spread/pallas_call | solution.py:257
  20.3 12.0 %all-to-all-start = ((bf16[128,4,32,128]{3,2,1,0:T(8,128)(2,1)}), bf16[128,4,32,128]{3,2,1,0:T(8,128)(2,1)}, u32[]{:S(2)}, u32[]{:S(2)}) async-start(bf16[128,4,32,128]{3,2,1,0:T(8,128)(2,1)} %bitcast.10), calls=%async_computation | async-start | bytes 8388608 | tf_op jit(solution)/shard_map/all_to_all | solution.py:567
  32.3 186.8 %gather_tokens.1 = (bf16[4,4,4,2,64,4096]{5,4,3,2,1,0:T(8,128)(2,1)}, bf16[16,32,512]{2,1,0:T(8,128)(2,1)}) custom-call(bf16[64,4096]{1,0:T(8,128)(2,1)} %fusion.1.own_ref, bf16[16,32,512]{2,1,0:T(8,128)(2,1)} %bitcast.14), custom_call_target="tpu_custom_call" | custom-call | bytes 134217728 | tf_op jit(solution)/shard_map/gather_tokens/pallas_call | solution.py:222
  219.1 0.0 all-to-all-done.blocks_ref
  219.1 0.0 copy-start.2
  219.1 7.8 %all-to-all-start.1 = ((bf16[128,4,32,128]{3,2,1,0:T(8,128)(2,1)}), bf16[128,4,32,128]{3,2,1,0:T(8,128)(2,1)}, u32[]{:S(2)}, u32[]{:S(2)}) async-start(bf16[128,4,32,128]{3,2,1,0:T(8,128)(2,1)} %bitcast.9), calls=%async_computation.1 | async-start | bytes 8388608 | tf_op jit(solution)/shard_map/all_to_all | solution.py:567
  227.0 0.0 copy-done.2
  227.0 0.1 copy.11
  227.1 0.1 eq.46.lists_ref
  227.2 0.0 copy-start.1
  227.2 0.7 convert_reduce_fusion.counts_ref
  227.8 0.9 fusion.2.swap_ref
  228.8 6.2 %gather_columns.1.table_ref = bf16[16,32,4096]{2,1,0:T(8,128)(2,1)} custom-call(bf16[128,4,32,128]{3,2,1,0:T(8,128)(2,1)} %all-to-all-done.blocks_ref, bf16[512,512]{1,0:T(8,128)(2,1)} %fusion.2.swap_ref), custom_call_target="tpu_custom_call" | custom-call | tf_op jit(solution)/shard_map/gather_columns/pallas_call | solution.py:307
  235.0 0.0 copy-done.1
  235.0 80.0 %inner_steps.1.sums_ref = f32[16,32,4096]{2,1,0:T(8,128)} custom-call(s32[32]{0:T(128)} %copy-done.1, bf16[8192,4096]{1,0:T(8,128)(2,1)} %bitcast.5.normed_ref, bf16[16,32,512]{2,1,0:T(8,128)(2,1)} %get-tuple-element.19.goal_ref, bf16[16,32,4096]{2,1,0:T(8,128)(2,1)} %gather_columns.1.table_ref), custom_call_target="tpu_custom_call" | custom-call | flops 34359738368 | bytes 67108864 | tf_op jit(solution)/shard_map/inner_steps/pallas_call | solution.py:457
  314.9 0.0 all-to-all-done.1.speed_ref
  314.9 12.1 %outer_step.1 = (bf16[16,32,4096]{2,1,0:T(8,128)(2,1)}, bf16[128,4,32,128]{3,2,1,0:T(8,128)(2,1)}) custom-call(f32[16]{0:T(128)} %convert_reduce_fusion.counts_ref, f32[16,32,4096]{2,1,0:T(8,128)} %inner_steps.1.sums_ref, bf16[16,32,4096]{2,1,0:T(8,128)(2,1)} %gather_columns.1.table_ref, bf16[128,4,32,128]{3,2,1,0:T(8,128)(2,1)} %all-to-all-done.1.speed_ref, ...), custom_call_target="tpu_custom_call" | custom-call | tf_op jit(solution)/shard_map/outer_step/pallas_call | solution.py:358
  327.1 10.2 %all-to-all-start.2 = ((bf16[128,4,32,128]{3,2,1,0:T(8,128)(2,1)}), bf16[128,4,32,128]{3,2,1,0:T(8,128)(2,1)}, u32[]{:S(2)}, u32[]{:S(2)}) async-start(bf16[128,4,32,128]{3,2,1,0:T(8,128)(2,1)} %get-tuple-element.22), calls=%async_computation.2 | async-start | bytes 8388608 | tf_op jit(solution)/shard_map/all_to_all | solution.py:567
  337.3 50.4 %evaluate.1 = bf16[512,512]{1,0:T(8,128)(2,1)} custom-call(s32[32]{0:T(128)} %copy-done.1, bf16[8192,4096]{1,0:T(8,128)(2,1)} %bitcast.5.normed_ref, bf16[16,32,4096]{2,1,0:T(8,128)(2,1)} %get-tuple-element.23.table_ref), custom_call_target="tpu_custom_call" | custom-call | flops 4294967296 | bytes 67108864 | tf_op jit(solution)/shard_map/evaluate/pallas_call | solution.py:539
  387.7 2.7 all-to-all-done.2
  390.4 0.0 copy-start
  390.4 7.2 %unspread.1 = bf16[4,128,4096]{2,1,0:T(8,128)(2,1)} custom-call(bf16[16,8,4,32,128]{4,3,2,1,0:T(8,128)(2,1)} %bitcast.7.blocks_ref), custom_call_target="tpu_custom_call" | custom-call | tf_op jit(solution)/shard_map/unspread/pallas_call | solution.py:276
  397.7 0.0 copy-done
  397.7 0.8 copy.14
  (2 shorter events, 0.0 us)
Async XLA Ops:
  20.3 198.8 %all-to-all-start = ((bf16[128,4,32,128]{3,2,1,0:T(8,128)(2,1)}), bf16[128,4,32,128]{3,2,1,0:T(8,128)(2,1)}, u32[]{:S(2)}, u32[]{:S(2)}) async-start(bf16[128,4,32,128]{3,2,1,0:T(8,128)(2,1)} %bitcast.10), calls=%async_computation | async-start | bytes 8388608 | tf_op jit(solution)/shard_map/all_to_all | solution.py:567
  219.1 7.9 %copy-start.2 = (s32[16,2]{0,1:T(2,128)S(1)}, s32[16,2]{0,1:T(2,128)}, u32[]{:S(2)}) copy-start(s32[16,2]{0,1:T(2,128)} %param.9) | copy-start | bytes 388
  219.1 95.8 %all-to-all-start.1 = ((bf16[128,4,32,128]{3,2,1,0:T(8,128)(2,1)}), bf16[128,4,32,128]{3,2,1,0:T(8,128)(2,1)}, u32[]{:S(2)}, u32[]{:S(2)}) async-start(bf16[128,4,32,128]{3,2,1,0:T(8,128)(2,1)} %bitcast.9), calls=%async_computation.1 | async-start | bytes 8388608 | tf_op jit(solution)/shard_map/all_to_all | solution.py:567
  227.2 7.8 %copy-start.1 = (s32[32]{0:T(128)}, s32[32]{0:T(128)S(1)}, u32[]{:S(2)}) copy-start(s32[32]{0:T(128)S(1)} %eq.46.lists_ref) | copy-start | bytes 388
  327.1 63.3 %all-to-all-start.2 = ((bf16[128,4,32,128]{3,2,1,0:T(8,128)(2,1)}), bf16[128,4,32,128]{3,2,1,0:T(8,128)(2,1)}, u32[]{:S(2)}, u32[]{:S(2)}) async-start(bf16[128,4,32,128]{3,2,1,0:T(8,128)(2,1)} %get-tuple-element.22), calls=%async_computation.2 | async-start | bytes 8388608 | tf_op jit(solution)/shard_map/all_to_all | solution.py:567
  390.4 7.2 %copy-start = (bf16[512,512]{1,0:T(8,128)(2,1)S(1)}, bf16[512,512]{1,0:T(8,128)(2,1)}, u32[]{:S(2)}) copy-start(bf16[512,512]{1,0:T(8,128)(2,1)} %evaluate.1) | copy-start | bytes 1572868

commit v4 on v3

--- a/solution.py
+++ b/solution.py
@@ -31,7 +31,47 @@
 ARRIVALS = 9
 
 
-def gather_tokens_kernel(own_ref, goal_ref, out_ref, goals_ref, local_sem, send_sem, recv_sem, goal_sem, goals_sem):
+def swap_values():
+    source = lax.broadcasted_iota(jnp.int32, (512, 512), 0)
+    target = lax.broadcasted_iota(jnp.int32, (512, 512), 1)
+    moved = ((source >> 5) & 3) * 128 + (source >> 7) * 32 + (source & 31)
+    return (moved == target).astype(jnp.float32).astype(jnp.bfloat16)
+
+
+def turn_out(rows_ref, blocks_ref, shards, paths):
+    groups, cols = blocks_ref.shape[1:3]
+    wide = paths * cols
+
+    @pl.loop(0, shards)
+    def _(shard):
+        columns = pl.ds(pl.multiple_of(shard * wide, wide), wide)
+        for g in range(groups):
+            turned = rows_ref[g, :, columns].T.reshape(paths, cols, 128)
+            for p in range(paths):
+                blocks_ref[p * shards + shard, g] = turned[p]
+
+
+def turn_in(blocks_ref, swap_ref, out_ref):
+    devices, groups, cols, _ = blocks_ref.shape
+    chunk = 8
+
+    @pl.loop(0, groups)
+    def _(g):
+        for begin in range(0, devices // 4, chunk):
+            blocks = blocks_ref[4 * begin : 4 * (begin + chunk), g].reshape(chunk, 4, cols, 128)
+            line = jnp.concatenate([blocks[:, s].reshape(chunk * cols, 128) for s in range(4)], axis=1)
+            turned = jnp.dot(line, swap_ref[...], preferred_element_type=jnp.float32)
+            turned = turned.astype(jnp.bfloat16).reshape(chunk, cols, 512)
+            for k in range(chunk):
+                columns = slice((begin + k) * 128, (begin + k + 1) * 128)
+                for q in range(4):
+                    out_ref[4 * g + q, :, columns] = turned[k, :, q * 128 : (q + 1) * 128]
+
+
+def gather_tokens_kernel(
+    own_ref, goal_ref, rows_ref, speed_ref, out_ref, goals_ref, table_ref, turned_ref,
+    rows_in, rows_out, turned, blocks_in, columns_of, swap, local_sem, send_sem, recv_sem, goal_sem, goals_sem, block_sem, blocks_sem, side_sem,
+):
     path, shard = lax.axis_index("path"), lax.axis_index("mp")
     me = {"z": path // RING, "y": path % RING, "x": shard // 2}
     core = shard % 2
@@ -43,14 +83,22 @@
         return (at["z"] * RING + at["y"], at["x"] * 2 + which)
 
     everyone = [device(shifted(axis, step), core) for axis in "xyz" for step in (1, -1)]
-    everyone.append(device(me, 1 - core))
-    paths = goal_ref.shape[0]
+    paths, shards = goal_ref.shape[0], out_ref.shape[2] * 2
     peers = [((path + step) % paths, shard) for step in range(1, paths)]
-    everyone += peers
+    devices = paths * shards
+    mine = path * shards + shard
+    load_rows = pltpu.make_async_copy(rows_ref, rows_in, side_sem.at[0])
+    load_rows.start()
     barrier = pltpu.get_barrier_semaphore()
-    for other in everyone:
-        pl.semaphore_signal(barrier, inc=1, device_id=other, device_id_type=pl.DeviceIdType.MESH)
-    pl.semaphore_wait(barrier, len(everyone))
+
+    @pl.loop(1, devices)
+    def _(step):
+        other = (mine + step) % devices
+        pl.semaphore_signal(
+            barrier, inc=1, device_id=(other // shards, other % shards), device_id_type=pl.DeviceIdType.MESH
+        )
+
+    pl.semaphore_wait(barrier, devices - 1)
 
     whole = pl.ds(0, RING)
     rows = own_ref.shape[0]
@@ -105,6 +153,42 @@
         first[part] = [
             send(me, device(shifted(a, step), core), full, columns, source) for step in (1, -1)
         ]
+    swap[...] = swap_values()
+    load_rows.wait()
+    turn_out(rows_in, rows_out, shards, paths)
+    own_block = pltpu.make_async_copy(rows_out.at[mine], blocks_in.at[mine], side_sem.at[1])
+    own_block.start()
+
+    def exchange_blocks(batch):
+        first = batch * BATCH
+
+        @pl.loop(max(first, 1), min(first + BATCH, devices))
+        def _(step):
+            other = (mine + step) % devices
+            pltpu.make_async_remote_copy(
+                src_ref=rows_out.at[other],
+                dst_ref=blocks_in.at[mine],
+                send_sem=block_sem.at[batch],
+                recv_sem=blocks_sem.at[batch],
+                device_id=(other // shards, other % shards),
+                device_id_type=pl.DeviceIdType.MESH,
+            ).start()
+
+    def exchanged(batch):
+        amount = BATCH - 1 if batch == 0 else BATCH
+        return pltpu.make_async_remote_copy(
+            src_ref=rows_out.at[pl.ds(0, amount)],
+            dst_ref=blocks_in.at[pl.ds(0, amount)],
+            send_sem=block_sem.at[batch],
+            recv_sem=blocks_sem.at[batch],
+            device_id=peers[0],
+            device_id_type=pl.DeviceIdType.MESH,
+        )
+
+    batches = devices // BATCH
+
+    for batch in range(batches):
+        exchange_blocks(batch)
     own_copy.wait()
 
     own_goal = pltpu.make_async_copy(goal_ref.at[path], goals_ref.at[path], goals_sem.at[0])
@@ -144,6 +228,9 @@
         arrived(halves[part, 0], origin, low, columns)
         arrived(halves[part, 1], origin, high, columns)
         second[part].append(send_both(origin, b, columns))
+
+    load_speed = pltpu.make_async_copy(speed_ref, rows_in, side_sem.at[0])
+    load_speed.start()
 
     third = {part: [] for part in range(len(PARTS))}
     for part, (a, b, c, begin, end) in enumerate(PARTS):
@@ -179,6 +266,18 @@
         share(line, columns)
 
     for unit in range(RING):
+        if unit == 1:
+            load_speed.wait()
+            turn_out(rows_in, turned, shards, paths)
+            store_speed = pltpu.make_async_copy(turned, turned_ref, side_sem.at[0])
+            store_speed.start()
+        if unit == 3:
+            own_block.wait()
+            for batch in range(batches):
+                exchanged(batch).wait_recv()
+            turn_in(blocks_in, swap, columns_of)
+            store_table = pltpu.make_async_copy(columns_of, table_ref, side_sem.at[1])
+            store_table.start()
         for index, step in ((0, 1), (1, -1)):
             lines = low if index == 0 else high
             for part, (a, b, c, begin, end) in enumerate(PARTS):
@@ -196,6 +295,10 @@
             share(far, columns)
     for number, at, columns in sibling_arrivals:
         arrived(number, at, full, columns, 1 - core)
+    for batch in range(batches):
+        exchanged(batch).wait_send()
+    store_speed.wait()
+    store_table.wait()
     own_goal.wait()
     for step, copy in enumerate(goal_copies, 1):
         copy.wait_send()
@@ -213,56 +316,51 @@
 
 
 COPIES = 156
-
-
-def gather_tokens(own, goal):
+BATCH = 16
+
+
+def gather_tokens(own, goal, table, speed):
     rows, width = own.shape
+    modules, rows_own, _ = table.shape
     paths, shards = lax.axis_size("path"), lax.axis_size("mp")
+    groups, cols = modules * rows_own // 128, width // (paths * shards)
     anywhere = pl.BlockSpec(memory_space=pl.ANY)
-    out, goals = pl.pallas_call(
+    blocks = (paths * shards, groups, cols, 128)
+    out, goals, table, speed = pl.pallas_call(
         gather_tokens_kernel,
-        in_specs=[anywhere, anywhere],
-        out_specs=[anywhere, anywhere],
+        in_specs=[anywhere] * 4,
+        out_specs=[anywhere] * 4,
         out_shape=[
             jax.ShapeDtypeStruct((paths // RING, RING, shards // 2, 2, rows, width), own.dtype),
             jax.ShapeDtypeStruct(goal.shape, goal.dtype),
+            jax.ShapeDtypeStruct((modules, cols, width), table.dtype),
+            jax.ShapeDtypeStruct(blocks, speed.dtype),
         ],
         scratch_shapes=[
+            pltpu.VMEM((groups, 128, width), table.dtype),
+            pltpu.VMEM(blocks, table.dtype),
+            pltpu.VMEM(blocks, table.dtype),
+            pltpu.VMEM(blocks, table.dtype),
+            pltpu.VMEM((modules, cols, width), table.dtype),
+            pltpu.VMEM((512, 512), jnp.bfloat16),
             pltpu.SemaphoreType.DMA,
             pltpu.SemaphoreType.DMA((COPIES,)),
             pltpu.SemaphoreType.DMA((COPIES,)),
             pltpu.SemaphoreType.DMA((paths,)),
             pltpu.SemaphoreType.DMA((paths,)),
+            pltpu.SemaphoreType.DMA((paths * shards // BATCH,)),
+            pltpu.SemaphoreType.DMA((paths * shards // BATCH,)),
+            pltpu.SemaphoreType.DMA((2,)),
         ],
-        compiler_params=pltpu.CompilerParams(collective_id=0, has_side_effects=True),
+        compiler_params=pltpu.CompilerParams(
+            vmem_limit_bytes=VMEM_LIMIT, collective_id=0, has_side_effects=True
+        ),
         cost_estimate=pl.CostEstimate(
             flops=0, bytes_accessed=4 * paths * shards * rows * width, transcendentals=0
         ),
         name="gather_tokens",
-    )(own, goal)
-    return out.reshape(paths * shards * rows, width), goals
-
-
-def spread_kernel(table_ref, out_ref):
-    for g in range(4):
-        turned = table_ref[g].T
-        out_ref[:, 0, g] = turned.reshape(out_ref.shape[0], out_ref.shape[3], 128)
-
-
-def spread(table, paths, shards):
-    modules, rows, width = table.shape
-    groups = modules * rows // 128
-    wide = width // shards
-    cols = wide // paths
-    return pl.pallas_call(
-        spread_kernel,
-        grid=(shards,),
-        in_specs=[pl.BlockSpec((groups, 128, wide), lambda i: (0, 0, i))],
-        out_specs=pl.BlockSpec((paths, 1, groups, cols, 128), lambda i: (0, i, 0, 0, 0)),
-        out_shape=jax.ShapeDtypeStruct((paths, shards, groups, cols, 128), table.dtype),
-        compiler_params=pltpu.CompilerParams(vmem_limit_bytes=VMEM_LIMIT),
-        name="spread",
-    )(table.reshape(groups, 128, width))
+    )(own, goal, table.reshape(groups, 128, width), speed.reshape(groups, 128, width))
+    return out.reshape(paths * shards * rows, width), goals, table, speed
 
 
 def unspread_kernel(blocks_ref, out_ref):
@@ -289,33 +387,6 @@
     index = jnp.arange(512)
     source, module, row = index // 128, (index // 32) % 4, index % 32
     return (index[:, None] == (module * 128 + source * 32 + row)[None, :]).astype(jnp.bfloat16)
-
-
-def gather_kernel(blocks_ref, swap_ref, out_ref):
-    quads, cols = blocks_ref.shape[0] // 4, blocks_ref.shape[2]
-    blocks = blocks_ref[:, 0].reshape(quads, 4, cols, 128)
-    line = jnp.concatenate([blocks[:, s].reshape(quads * cols, 128) for s in range(4)], axis=1)
-    turned = jnp.dot(line, swap_ref[...], preferred_element_type=jnp.float32).astype(jnp.bfloat16)
-    turned = turned.reshape(quads, cols, 512)
-    for k in range(quads):
-        for q in range(4):
-            out_ref[q, :, k * 128 : (k + 1) * 128] = turned[k, :, q * 128 : (q + 1) * 128]
-
-
-def gather_columns(blocks):
-    devices, groups, cols, _ = blocks.shape
-    return pl.pallas_call(
-        gather_kernel,
-        grid=(groups,),
-        in_specs=[
-            pl.BlockSpec((devices, 1, cols, 128), lambda g: (0, g, 0, 0)),
-            pl.BlockSpec((512, 512), lambda g: (0, 0)),
-        ],
-        out_specs=pl.BlockSpec((4, cols, devices * 32), lambda g: (g, 0, 0)),
-        out_shape=jax.ShapeDtypeStruct((groups * 4, cols, devices * 32), blocks.dtype),
-        compiler_params=pltpu.CompilerParams(vmem_limit_bytes=VMEM_LIMIT),
-        name="gather_columns",
-    )(blocks, swap_matrix())
 
 
 CHUNK = 8
@@ -398,7 +469,7 @@
 TILE = 512
 
 
-def inner_kernel(lists_ref, normed_ref, goal_ref, table_ref, sums_ref, start, current, first_grad, slope, turned):
+def inner_kernel(lists_ref, normed_ref, goal_ref, table_ref, sums_ref, start, current, first_grad, master, slope, turned):
     path = pl.program_id(0)
     gate, up = lists_ref[2 * path], lists_ref[2 * path + 1]
     cols = goal_ref.shape[1]
@@ -411,43 +482,49 @@
     start[:cols] = table_ref[gate]
     start[cols:] = table_ref[up]
     goal = goal_ref[0].astype(jnp.float32)
-    for j in range(width // TILE):
-        turned[j * TILE : (j + 1) * TILE, :] = normed_ref[:, j * TILE : (j + 1) * TILE].T
+    for j in range(width // 512):
+        turned[j * 512 : (j + 1) * 512, :] = normed_ref[:, j * 512 : (j + 1) * 512].T
     slope[...] = slopes(start[...], turned[...], goal)
 
     def product(columns):
         parts = jnp.dot(slope[...], normed_ref[:, columns], preferred_element_type=jnp.float32)
         return parts[: 2 * cols] + (parts[2 * cols : 4 * cols] + parts[4 * cols :])
 
-    def after_first(begin, grad):
-        return begin - inner_rate * (grad / (jnp.abs(grad) + adam_epsilon) + weight_decay * begin)
-
-    for j in range(width // TILE):
-        columns = slice(j * TILE, (j + 1) * TILE)
-        grad = product(columns)
+    def sweep(update):
+        tiles = [slice(j * TILE, (j + 1) * TILE) for j in range(width // TILE)]
+        grad = product(tiles[0])
+        for this, following in zip(tiles, tiles[1:] + [None]):
+            later = product(following) if following is not None else None
+            update(this, grad)
+            grad = later
+
+    def first_step(columns, grad):
         first_grad[:, columns] = grad
         begin = start[:, columns].astype(jnp.float32)
-        current[:, columns] = after_first(begin, grad).astype(jnp.bfloat16)
-
-    slope[...] = slopes(current[...], turned[...], goal)
-    for j in range(width // TILE):
-        columns = slice(j * TILE, (j + 1) * TILE)
-        grad = product(columns)
+        after = begin - inner_rate * (grad / (jnp.abs(grad) + adam_epsilon) + weight_decay * begin)
+        master[:, columns] = after
+        current[:, columns] = after.astype(jnp.bfloat16)
+
+    def second_step(columns, grad):
         before = first_grad[:, columns]
         begin = start[:, columns].astype(jnp.float32)
-        master = after_first(begin, before)
+        after = master[:, columns]
         first = (beta_first * (1.0 - beta_first) / (1.0 - beta_first**2)) * before + (
             (1.0 - beta_first) / (1.0 - beta_first**2)
         ) * grad
         second = (beta_second * (1.0 - beta_second) / (1.0 - beta_second**2)) * before * before + (
             (1.0 - beta_second) / (1.0 - beta_second**2)
         ) * grad * grad
-        master = master - inner_rate * (
-            first / (jnp.sqrt(second) + adam_epsilon) + weight_decay * master
+        after = after - inner_rate * (
+            first / (jnp.sqrt(second) + adam_epsilon) + weight_decay * after
         )
-        delta = (begin - master).astype(jnp.bfloat16).astype(jnp.float32)
+        delta = (begin - after).astype(jnp.bfloat16).astype(jnp.float32)
         sums_ref[gate, :, columns] += delta[:cols]
         sums_ref[up, :, columns] += delta[cols:]
+
+    sweep(first_step)
+    slope[...] = slopes(current[...], turned[...], goal)
+    sweep(second_step)
 
 
 def inner_steps(lists, normed, goals, table):
@@ -468,6 +545,7 @@
             scratch_shapes=[
                 pltpu.VMEM((2 * cols, width), jnp.bfloat16),
                 pltpu.VMEM((2 * cols, width), jnp.bfloat16),
+                pltpu.VMEM((2 * cols, width), jnp.float32),
                 pltpu.VMEM((2 * cols, width), jnp.float32),
                 pltpu.VMEM((6 * cols, TOK_PATH), jnp.bfloat16),
                 pltpu.VMEM((width, TOK_PATH), jnp.bfloat16),
@@ -579,14 +657,8 @@
         return exchange(blocks.reshape((paths * shards,) + blocks.shape[-3:]), both)
 
     own, goal = normalize(features), targets.T.reshape(paths, cols, TOK_PATH)
-    speed, module_table, own, goal = lax.optimization_barrier(
-        (spread(momentum, paths, shards), spread(module_table, paths, shards), own, goal)
-    )
-    arrived = sent(module_table)
-    normed, goals = gather_tokens(own, goal)
-    arrived, normed, speed = lax.optimization_barrier((arrived, normed, speed))
+    normed, goals, table, speed = gather_tokens(own, goal, module_table, momentum)
     speed = sent(speed)
-    table = gather_columns(arrived)
     select = lists[None, :] == jnp.arange(modules, dtype=jnp.int32)[:, None]
     counts = jnp.sum(select.astype(jnp.float32), axis=1)
     sums = inner_steps(lists, normed, goals, table)

time: 403 us -> 395 us (0.980)
  starting transfers between devices: 30 us -> 17.5 us
  Pallas kernels: 357 us -> 363 us
    all_to_all x3 -> x2, starting transfers between devices: 30 us -> 17.5 us  [exchange(): return lax.all_to_all(blocks, axes, split_axis=0, concat_axis=0, tiled=True)]
    pallas_call x4 -> x1, Pallas kernels: 207 us -> 213 us  [gather_tokens(): pl.pallas_call(gather_tokens_kernel, in_specs=[anywhere] * 4, out_specs=[...]
  transfers between devices with their start and end apart: 3 -> 2, of which waited for: 1 -> 1; matrix products, arithmetic and copies ran while one was open for 0% -> 0% of each run, Pallas kernels for 81% -> 33%
where the time goes in v4:
time: 395 us; the launch traced here: 391 us
  Pallas kernels  363 us (92%)
  starting transfers between devices  17.5 us (4%)
  other arithmetic  4.83 us (1%)
    pallas_call x1, Pallas kernels, gather_tokens(): pl.pallas_call(gather_tokens_kernel, in_specs=[anywhere] * 4, out_specs=[...  213 us
    pallas_call x1, Pallas kernels, inner_steps(): pl.pallas_call(inner_kernel, grid_spec=pltpu.PrefetchScalarGridSpec(num_s...  79.9 us
    pallas_call x1, Pallas kernels, evaluate(): pl.pallas_call(evaluate_kernel, grid=(paths,), in_specs=[pl.BlockSpec(mem...  50.4 us
    all_to_all x2, starting transfers between devices, exchange(): return lax.all_to_all(blocks, axes, split_axis=0, concat_axis=0, tiled=True)  17.5 us
    pallas_call x1, Pallas kernels, outer_step(): pl.pallas_call(outer_kernel, grid=(groups,), in_specs=[pl.BlockSpec(memor...  12.1 us
  transfers between devices with their start and end apart: 2, of which 1 were waited for; matrix products, arithmetic and copies ran while one was open for 0% of the time, Pallas kernels for 33%

profile of v4, /device:TPU:1, one launch (start us, length us, event | category | flops | bytes accessed | tf_op | source)
XLA Modules:
  0.0 391.5 jit_solution(9234330284943741323)
XLA Ops:
  0.6 1.2 fusion
  1.9 2.0 fusion.1.own_ref
  3.9 2.0 copy.12
  5.9 213.0 %gather_tokens.1 = (bf16[4,4,4,2,64,4096]{5,4,3,2,1,0:T(8,128)(2,1)}, bf16[16,32,512]{2,1,0:T(8,128)(2,1)}, bf16[16,32,4096]{2,1,0:T(8,128)(2,1)}, bf16[128,4,32,128]{3,2,1,0:T(8,128)(2,1)}) custom-call(bf16[64,4096]{1,0:T(8,128)(2,1)} %fusion.1.own_ref, bf16[16,32,512]{2,1,0:T(8,128)(2,1)} %bitcast.10, bf16[4,128,4096]{2,1,0:T(8,128)(2,1)} %bitcast.7, ...), custom_call_target="tpu_custom_call" | custom-call | bytes 134217728 | tf_op jit(solution)/shard_map/gather_tokens/pallas_call | solution.py:329
  218.9 0.0 copy-start.2
  218.9 7.3 %all-to-all-start = ((bf16[128,4,32,128]{3,2,1,0:T(8,128)(2,1)}), bf16[128,4,32,128]{3,2,1,0:T(8,128)(2,1)}, u32[]{:S(2)}, u32[]{:S(2)}) async-start(bf16[128,4,32,128]{3,2,1,0:T(8,128)(2,1)} %get-tuple-element.11), calls=%async_computation | async-start | bytes 8388608 | tf_op jit(solution)/shard_map/all_to_all | solution.py:645
  226.2 0.0 copy-done.2
  226.2 0.1 copy.11
  226.3 0.1 eq.31.lists_ref
  226.4 0.0 copy-start.1
  226.4 0.7 convert_reduce_fusion.counts_ref
  227.1 0.9 fusion.2.swap_ref
  228.0 0.0 copy-done.1
  228.0 79.9 %inner_steps.1.sums_ref = f32[16,32,4096]{2,1,0:T(8,128)} custom-call(s32[32]{0:T(128)} %copy-done.1, bf16[8192,4096]{1,0:T(8,128)(2,1)} %bitcast.4.normed_ref, bf16[16,32,512]{2,1,0:T(8,128)(2,1)} %get-tuple-element.9.goal_ref, bf16[16,32,4096]{2,1,0:T(8,128)(2,1)} %get-tuple-element.10.table_ref), custom_call_target="tpu_custom_call" | custom-call | flops 34359738368 | bytes 67108864 | tf_op jit(solution)/shard_map/inner_steps/pallas_call | solution.py:534
  308.0 0.0 all-to-all-done.speed_ref
  308.0 12.1 %outer_step.1 = (bf16[16,32,4096]{2,1,0:T(8,128)(2,1)}, bf16[128,4,32,128]{3,2,1,0:T(8,128)(2,1)}) custom-call(f32[16]{0:T(128)} %convert_reduce_fusion.counts_ref, f32[16,32,4096]{2,1,0:T(8,128)} %inner_steps.1.sums_ref, bf16[16,32,4096]{2,1,0:T(8,128)(2,1)} %get-tuple-element.10.table_ref, bf16[128,4,32,128]{3,2,1,0:T(8,128)(2,1)} %all-to-all-done.speed_ref, ...), custom_call_target="tpu_custom_call" | custom-call | tf_op jit(solution)/shard_map/outer_step/pallas_call | solution.py:429
  320.1 10.2 %all-to-all-start.1 = ((bf16[128,4,32,128]{3,2,1,0:T(8,128)(2,1)}), bf16[128,4,32,128]{3,2,1,0:T(8,128)(2,1)}, u32[]{:S(2)}, u32[]{:S(2)}) async-start(bf16[128,4,32,128]{3,2,1,0:T(8,128)(2,1)} %get-tuple-element.12), calls=%async_computation.1 | async-start | bytes 8388608 | tf_op jit(solution)/shard_map/all_to_all | solution.py:645
  330.3 50.4 %evaluate.1 = bf16[512,512]{1,0:T(8,128)(2,1)} custom-call(s32[32]{0:T(128)} %copy-done.1, bf16[8192,4096]{1,0:T(8,128)(2,1)} %bitcast.4.normed_ref, bf16[16,32,4096]{2,1,0:T(8,128)(2,1)} %get-tuple-element.13.table_ref), custom_call_target="tpu_custom_call" | custom-call | flops 4294967296 | bytes 67108864 | tf_op jit(solution)/shard_map/evaluate/pallas_call | solution.py:617
  380.7 2.7 all-to-all-done.1
  383.4 0.0 copy-start
  383.4 7.2 %unspread.1 = bf16[4,128,4096]{2,1,0:T(8,128)(2,1)} custom-call(bf16[16,8,4,32,128]{4,3,2,1,0:T(8,128)(2,1)} %bitcast.5.blocks_ref), custom_call_target="tpu_custom_call" | custom-call | tf_op jit(solution)/shard_map/unspread/pallas_call | solution.py:374
  390.7 0.0 copy-done
  390.7 0.8 copy.14
  (2 shorter events, 0.0 us)
Async XLA Ops:
  218.9 7.3 %copy-start.2 = (s32[16,2]{0,1:T(2,128)S(1)}, s32[16,2]{0,1:T(2,128)}, u32[]{:S(2)}) copy-start(s32[16,2]{0,1:T(2,128)} %param.9) | copy-start | bytes 388
  218.9 89.0 %all-to-all-start = ((bf16[128,4,32,128]{3,2,1,0:T(8,128)(2,1)}), bf16[128,4,32,128]{3,2,1,0:T(8,128)(2,1)}, u32[]{:S(2)}, u32[]{:S(2)}) async-start(bf16[128,4,32,128]{3,2,1,0:T(8,128)(2,1)} %get-tuple-element.11), calls=%async_computation | async-start | bytes 8388608 | tf_op jit(solution)/shard_map/all_to_all | solution.py:645
  226.4 1.6 copy-start.1
  320.1 63.4 %all-to-all-start.1 = ((bf16[128,4,32,128]{3,2,1,0:T(8,128)(2,1)}), bf16[128,4,32,128]{3,2,1,0:T(8,128)(2,1)}, u32[]{:S(2)}, u32[]{:S(2)}) async-start(bf16[128,4,32,128]{3,2,1,0:T(8,128)(2,1)} %get-tuple-element.12), calls=%async_computation.1 | async-start | bytes 8388608 | tf_op jit(solution)/shard_map/all_to_all | solution.py:645
  383.4 7.2 %copy-start = (bf16[512,512]{1,0:T(8,128)(2,1)S(1)}, bf16[512,512]{1,0:T(8,128)(2,1)}, u32[]{:S(2)}) copy-start(bf16[512,512]{1,0:T(8,128)(2,1)} %evaluate.1) | copy-start | bytes 1572868

commit v5 on v4

--- a/solution.py
+++ b/solution.py
@@ -93,7 +93,7 @@
 
     @pl.loop(1, devices)
     def _(step):
-        other = (mine + step) % devices
+        other = (mine + 37 * step) % devices
         pl.semaphore_signal(
             barrier, inc=1, device_id=(other // shards, other % shards), device_id_type=pl.DeviceIdType.MESH
         )
@@ -164,7 +164,7 @@
 
         @pl.loop(max(first, 1), min(first + BATCH, devices))
         def _(step):
-            other = (mine + step) % devices
+            other = (mine + 37 * step) % devices
             pltpu.make_async_remote_copy(
                 src_ref=rows_out.at[other],
                 dst_ref=blocks_in.at[mine],
@@ -392,58 +392,32 @@
 CHUNK = 8
 
 
-def outer_kernel(counts_ref, sums_ref, table_ref, speed_ref, swap_ref, updated_ref, out_ref):
-    group = pl.program_id(0)
+def outer_step(counts_ref, sums_ref, table_ref, speed_ref, swap_ref, updated_ref, out_ref, group):
     quads, cols = out_ref.shape[0] // 4, out_ref.shape[2]
     counts = [counts_ref[4 * group + q] for q in range(4)]
     for begin in range(0, quads, CHUNK):
-        blocks = speed_ref[4 * begin : 4 * (begin + CHUNK), 0].reshape(CHUNK, 4, cols, 128)
+        blocks = speed_ref[4 * begin : 4 * (begin + CHUNK), group].reshape(CHUNK, 4, cols, 128)
         line = jnp.concatenate([blocks[:, s].reshape(CHUNK * cols, 128) for s in range(4)], axis=1)
         speed = jnp.dot(line, swap_ref[...], preferred_element_type=jnp.float32).reshape(CHUNK, cols, 512)
         lines = []
         for k in range(CHUNK):
-            pieces_of = []
+            moments = []
             for q in range(4):
                 columns = slice((begin + k) * 128, (begin + k + 1) * 128)
-                average = sums_ref[q, :, columns] / counts[q]
+                average = sums_ref[4 * group + q, :, columns] / counts[q]
                 moment = outer_momentum * speed[k, :, q * 128 : (q + 1) * 128] + average
-                begun = table_ref[q, :, columns].astype(jnp.float32)
-                updated_ref[q, :, columns] = (
+                begun = table_ref[4 * group + q, :, columns].astype(jnp.float32)
+                updated_ref[4 * group + q, :, columns] = (
                     begun - outer_rate * (average + outer_momentum * moment)
                 ).astype(jnp.bfloat16)
-                pieces_of.append(moment.astype(jnp.bfloat16))
-            lines.append(jnp.concatenate(pieces_of, axis=1))
+                moments.append(moment.astype(jnp.bfloat16))
+            lines.append(jnp.concatenate(moments, axis=1))
         line = jnp.concatenate(lines, axis=0)
         turned = jnp.dot(line, swap_ref[...], preferred_element_type=jnp.float32).astype(jnp.bfloat16)
         turned = turned.reshape(CHUNK, cols, 512)
         for k in range(CHUNK):
             for s in range(4):
-                out_ref[4 * (begin + k) + s, 0] = turned[k, :, s * 128 : (s + 1) * 128]
-
-
-def outer_step(counts, sums, table, speed):
-    modules, cols, width = table.shape
-    devices, groups = speed.shape[:2]
-    rows = pl.BlockSpec((4, cols, width), lambda g: (g, 0, 0))
-    blocks = pl.BlockSpec((devices, 1, cols, 128), lambda g: (0, g, 0, 0))
-    return pl.pallas_call(
-        outer_kernel,
-        grid=(groups,),
-        in_specs=[
-            pl.BlockSpec(memory_space=pltpu.SMEM),
-            rows,
-            rows,
-            blocks,
-            pl.BlockSpec((512, 512), lambda g: (0, 0)),
-        ],
-        out_specs=[rows, blocks],
-        out_shape=[
-            jax.ShapeDtypeStruct(table.shape, table.dtype),
-            jax.ShapeDtypeStruct(speed.shape, speed.dtype),
-        ],
-        compiler_params=pltpu.CompilerParams(vmem_limit_bytes=VMEM_LIMIT),
-        name="outer_step",
-    )(counts, sums, table, speed, swap_matrix())
+                out_ref[4 * (begin + k) + s, group] = turned[k, :, s * 128 : (s + 1) * 128]
 
 
 def pieces(value):
@@ -560,7 +534,11 @@
     )(lists, normed, goals, table)
 
 
-def evaluate_kernel(lists_ref, normed_ref, table_ref, out_ref, weights, outgoing, arrived, send_sem, recv_sem):
+def finish_kernel(
+    lists_ref, counts_ref, normed_ref, sums_ref, table_ref, speed_ref, moments_ref, out_ref,
+    sums, begun, speed, updated, blocks_out, blocks_in, swap, weights, outgoing, arrived,
+    send_sem, recv_sem, block_sem, blocks_sem, sums_sem, side_sem,
+):
     target = pl.program_id(0)
     path, shard = lax.axis_index("path"), lax.axis_index("mp")
     paths, cols, tokens = arrived.shape
@@ -575,20 +553,73 @@
             device_id_type=pl.DeviceIdType.MESH,
         )
 
+    devices, groups = blocks_out.shape[:2]
+    shards = devices // paths
+    mine = path * shards + shard
+    batches = devices // BATCH
+
+    def exchanged(batch):
+        amount = BATCH - 1 if batch == 0 else BATCH
+        return pltpu.make_async_remote_copy(
+            src_ref=blocks_out.at[pl.ds(0, amount)],
+            dst_ref=blocks_in.at[pl.ds(0, amount)],
+            send_sem=block_sem.at[batch],
+            recv_sem=blocks_sem.at[batch],
+            device_id=((path + 1) % paths, shard),
+            device_id_type=pl.DeviceIdType.MESH,
+        )
+
+    def own_block():
+        return pltpu.make_async_copy(blocks_out.at[mine], blocks_in.at[mine], side_sem.at[0])
+
     @pl.when(target == 0)
     def _():
+        load_table = pltpu.make_async_copy(table_ref, begun, side_sem.at[0])
+        load_speed = pltpu.make_async_copy(speed_ref, speed, side_sem.at[1])
+        load_speed.start()
+        load_table.start()
+        loads = []
+        for g in range(groups):
+            part = pl.ds(4 * g, 4)
+            loads.append(pltpu.make_async_copy(sums_ref.at[part], sums.at[part], sums_sem.at[g]))
+            loads[-1].start()
         barrier = pltpu.get_barrier_semaphore()
-        for step in range(1, paths):
+
+        @pl.loop(1, devices)
+        def _(step):
+            other = (mine + 37 * step) % devices
             pl.semaphore_signal(
-                barrier,
-                inc=1,
-                device_id=((path + step) % paths, shard),
-                device_id_type=pl.DeviceIdType.MESH,
+                barrier, inc=1, device_id=(other // shards, other % shards), device_id_type=pl.DeviceIdType.MESH
             )
-        pl.semaphore_wait(barrier, paths - 1)
-
-    weights[:cols] = table_ref[lists_ref[2 * target]]
-    weights[cols:] = table_ref[lists_ref[2 * target + 1]]
+
+        swap[...] = swap_values()
+        load_speed.wait()
+        load_table.wait()
+        for load in loads:
+            load.wait()
+
+        @pl.loop(0, groups)
+        def _(group):
+            outer_step(counts_ref, sums, begun, speed, swap, updated, blocks_out, group)
+
+        own_block().start()
+        pl.semaphore_wait(barrier, devices - 1)
+        for batch in range(batches):
+
+            @pl.loop(max(batch * BATCH, 1), (batch + 1) * BATCH)
+            def _(step):
+                other = (mine + 37 * step) % devices
+                pltpu.make_async_remote_copy(
+                    src_ref=blocks_out.at[other],
+                    dst_ref=blocks_in.at[mine],
+                    send_sem=block_sem.at[batch],
+                    recv_sem=blocks_sem.at[batch],
+                    device_id=(other // shards, other % shards),
+                    device_id_type=pl.DeviceIdType.MESH,
+                ).start()
+
+    weights[:cols] = updated[lists_ref[2 * target]]
+    weights[cols:] = updated[lists_ref[2 * target + 1]]
     both = lax.dot_general(weights[...], normed_ref[...], NT, preferred_element_type=jnp.float32)
     gate_act = both[:cols]
     result = (gate_act * jax.nn.sigmoid(gate_act) * both[cols:]).astype(jnp.bfloat16)
@@ -608,37 +639,61 @@
             other = (path + step) % paths
             remote(other, other, other, other).wait()
         out_ref[...] = arrived[...].reshape(paths * cols, tokens).T
-
-
-def evaluate(lists, normed, table):
+        own_block().wait()
+        for batch in range(batches):
+            exchanged(batch).wait()
+        store = pltpu.make_async_copy(blocks_in, moments_ref, side_sem.at[0])
+        store.start()
+        store.wait()
+
+
+def finish(lists, counts, normed, sums, table, speed):
     modules, cols, width = table.shape
     tokens = normed.shape[0]
     paths = tokens // TOK_PATH
+    scalars, anywhere = pl.BlockSpec(memory_space=pltpu.SMEM), pl.BlockSpec(memory_space=pl.ANY)
     return pl.pallas_call(
-        evaluate_kernel,
+        finish_kernel,
         grid=(paths,),
         in_specs=[
-            pl.BlockSpec(memory_space=pltpu.SMEM),
+            scalars,
+            scalars,
             pl.BlockSpec((TOK_PATH, width), lambda p: (p, 0)),
-            pl.BlockSpec((modules, cols, width), lambda p: (0, 0, 0)),
+            anywhere,
+            anywhere,
+            anywhere,
         ],
-        out_specs=pl.BlockSpec((TOK_PATH, paths * cols), lambda p: (0, 0)),
+        out_specs=[anywhere, pl.BlockSpec((TOK_PATH, paths * cols), lambda p: (0, 0))],
         scratch_shapes=[
+            pltpu.VMEM(sums.shape, sums.dtype),
+            pltpu.VMEM(table.shape, table.dtype),
+            pltpu.VMEM(speed.shape, speed.dtype),
+            pltpu.VMEM(table.shape, table.dtype),
+            pltpu.VMEM(speed.shape, speed.dtype),
+            pltpu.VMEM(speed.shape, speed.dtype),
+            pltpu.VMEM((512, 512), jnp.bfloat16),
             pltpu.VMEM((2 * cols, width), jnp.bfloat16),
             pltpu.VMEM((paths, cols, TOK_PATH), jnp.bfloat16),
             pltpu.VMEM((paths, cols, TOK_PATH), jnp.bfloat16),
             pltpu.SemaphoreType.DMA((paths,)),
             pltpu.SemaphoreType.DMA((paths,)),
+            pltpu.SemaphoreType.DMA((speed.shape[0] // BATCH,)),
+            pltpu.SemaphoreType.DMA((speed.shape[0] // BATCH,)),
+            pltpu.SemaphoreType.DMA((speed.shape[1],)),
+            pltpu.SemaphoreType.DMA((2,)),
         ],
-        out_shape=jax.ShapeDtypeStruct((TOK_PATH, paths * cols), jnp.bfloat16),
+        out_shape=[
+            jax.ShapeDtypeStruct(speed.shape, speed.dtype),
+            jax.ShapeDtypeStruct((TOK_PATH, paths * cols), jnp.bfloat16),
+        ],
         compiler_params=pltpu.CompilerParams(
             vmem_limit_bytes=VMEM_LIMIT, collective_id=1, has_side_effects=True
         ),
         cost_estimate=pl.CostEstimate(
             flops=4 * tokens * width * cols, bytes_accessed=2 * tokens * width, transcendentals=0
         ),
-        name="evaluate",
-    )(lists, normed, table)
+        name="finish",
+    )(lists, counts, normed, sums, table, speed)
 
 
 def exchange(blocks, axes):
@@ -662,9 +717,7 @@
     select = lists[None, :] == jnp.arange(modules, dtype=jnp.int32)[:, None]
     counts = jnp.sum(select.astype(jnp.float32), axis=1)
     sums = inner_steps(lists, normed, goals, table)
-    updated, blocks = lax.optimization_barrier(outer_step(counts, sums, table, speed))
-    blocks = sent(blocks)
-    evaluated = evaluate(lists, normed, updated)
+    blocks, evaluated = finish(lists, counts, normed, sums, table, speed)
     momentum_out = unspread(blocks.reshape((paths, shards) + blocks.shape[1:]), modules, rows_own)
     return (momentum_out, evaluated)
 

time: 395 us -> 374 us (0.947)
  starting transfers between devices: 17.5 us -> 6.17 us
  Pallas kernels: 363 us -> 358 us
    pallas_call x1, Pallas kernels: 213 us -> 197 us  [gather_tokens(): pl.pallas_call(gather_tokens_kernel, in_specs=[anywhere] * 4, out_specs=[...]
    all_to_all x2 -> x1, starting transfers between devices: 17.5 us -> 6.17 us  [exchange(): return lax.all_to_all(blocks, axes, split_axis=0, concat_axis=0, tiled=True)]
    pallas_call x2 -> x1, Pallas kernels: 62.5 us -> 73.2 us  [finish(): pl.pallas_call(finish_kernel, grid=(paths,), in_specs=[scalars, scalars,...]
  transfers between devices with their start and end apart: 2 -> 1, of which waited for: 1 -> 0; matrix products, arithmetic and copies ran while one was open for 0% -> 0% of each run, Pallas kernels for 33% -> 22%
where the time goes in v5:
time: 374 us; the launch traced here: 372 us
  Pallas kernels  358 us (96%)
  starting transfers between devices  6.17 us (2%)
  other arithmetic  3.88 us (1%)
    pallas_call x1, Pallas kernels, gather_tokens(): pl.pallas_call(gather_tokens_kernel, in_specs=[anywhere] * 4, out_specs=[...  197 us
    pallas_call x1, Pallas kernels, inner_steps(): pl.pallas_call(inner_kernel, grid_spec=pltpu.PrefetchScalarGridSpec(num_s...  79.9 us
    pallas_call x1, Pallas kernels, finish(): pl.pallas_call(finish_kernel, grid=(paths,), in_specs=[scalars, scalars,...  73.2 us
  transfers between devices with their start and end apart: 1, of which 0 were waited for; matrix products, arithmetic and copies ran while one was open for 0% of the time, Pallas kernels for 22%

profile of v5, /device:TPU:1, one launch (start us, length us, event | category | flops | bytes accessed | tf_op | source)
XLA Modules:
  0.0 371.7 jit_solution(14593206935859524693)
XLA Ops:
  0.6 1.2 fusion
  1.9 2.0 fusion.1.own_ref
  3.9 2.0 copy.12
  5.9 197.5 %gather_tokens.1 = (bf16[4,4,4,2,64,4096]{5,4,3,2,1,0:T(8,128)(2,1)}, bf16[16,32,512]{2,1,0:T(8,128)(2,1)}, bf16[16,32,4096]{2,1,0:T(8,128)(2,1)}, bf16[128,4,32,128]{3,2,1,0:T(8,128)(2,1)}) custom-call(bf16[64,4096]{1,0:T(8,128)(2,1)} %fusion.1.own_ref, bf16[16,32,512]{2,1,0:T(8,128)(2,1)} %bitcast.11, bf16[4,128,4096]{2,1,0:T(8,128)(2,1)} %bitcast.7, ...), custom_call_target="tpu_custom_call" | custom-call | bytes 134217728 | tf_op jit(solution)/shard_map/gather_tokens/pallas_call | solution.py:329
  203.4 0.0 copy-start.2
  203.5 6.2 %all-to-all-start = ((bf16[128,4,32,128]{3,2,1,0:T(8,128)(2,1)}), bf16[128,4,32,128]{3,2,1,0:T(8,128)(2,1)}, u32[]{:S(2)}, u32[]{:S(2)}) async-start(bf16[128,4,32,128]{3,2,1,0:T(8,128)(2,1)} %get-tuple-element.11), calls=%async_computation | async-start | bytes 8388608 | tf_op jit(solution)/shard_map/all_to_all | solution.py:700
  209.6 0.0 copy-done.2
  209.6 0.1 copy.11
  209.7 0.1 reshape.34.lists_ref
  209.8 0.0 copy-start.1
  209.8 0.6 convert_reduce_fusion.counts_ref
  210.5 0.0 copy-done.1
  210.5 79.9 %inner_steps.1.sums_ref = f32[16,32,4096]{2,1,0:T(8,128)} custom-call(s32[32]{0:T(128)} %copy-done.1, bf16[8192,4096]{1,0:T(8,128)(2,1)} %bitcast.4.normed_ref, bf16[16,32,512]{2,1,0:T(8,128)(2,1)} %get-tuple-element.9.goal_ref, bf16[16,32,4096]{2,1,0:T(8,128)(2,1)} %get-tuple-element.10.table_ref), custom_call_target="tpu_custom_call" | custom-call | flops 34359738368 | bytes 67108864 | tf_op jit(solution)/shard_map/inner_steps/pallas_call | solution.py:508
  290.4 0.0 all-to-all-done.speed_ref
  290.4 73.2 %finish.1 = (bf16[128,4,32,128]{3,2,1,0:T(8,128)(2,1)}, bf16[512,512]{1,0:T(8,128)(2,1)}) custom-call(s32[32]{0:T(128)} %copy-done.1, f32[16]{0:T(128)} %convert_reduce_fusion.counts_ref, bf16[8192,4096]{1,0:T(8,128)(2,1)} %bitcast.4.normed_ref, f32[16,32,4096]{2,1,0:T(8,128)} %inner_steps.1.sums_ref, bf16[16,32,4096]{2,1,0:T(8,128)(2,1)} %get-tuple-element.10.table_ref, ...), custom_call_target="tpu_custom_call" | custom-call | flops 4294967296 | bytes 67108864 | tf_op jit(solution)/shard_map/finish/pallas_call | solution.py:655
  363.6 0.0 copy-start
  363.6 7.3 %unspread.1 = bf16[4,128,4096]{2,1,0:T(8,128)(2,1)} custom-call(bf16[16,8,4,32,128]{4,3,2,1,0:T(8,128)(2,1)} %bitcast.10), custom_call_target="tpu_custom_call" | custom-call | tf_op jit(solution)/shard_map/unspread/pallas_call | solution.py:374
  370.9 0.0 copy-done
  370.9 0.8 copy.14
  (1 shorter events, 0.0 us)
Async XLA Ops:
  203.4 6.2 %copy-start.2 = (s32[16,2]{0,1:T(2,128)S(1)}, s32[16,2]{0,1:T(2,128)}, u32[]{:S(2)}) copy-start(s32[16,2]{0,1:T(2,128)} %param.9) | copy-start | bytes 388
  203.5 86.9 %all-to-all-start = ((bf16[128,4,32,128]{3,2,1,0:T(8,128)(2,1)}), bf16[128,4,32,128]{3,2,1,0:T(8,128)(2,1)}, u32[]{:S(2)}, u32[]{:S(2)}) async-start(bf16[128,4,32,128]{3,2,1,0:T(8,128)(2,1)} %get-tuple-element.11), calls=%async_computation | async-start | bytes 8388608 | tf_op jit(solution)/shard_map/all_to_all | solution.py:700
  209.8 0.6 copy-start.1
  363.6 7.3 %copy-start = (bf16[512,512]{1,0:T(8,128)(2,1)S(1)}, bf16[512,512]{1,0:T(8,128)(2,1)}, u32[]{:S(2)}) copy-start(bf16[512,512]{1,0:T(8,128)(2,1)} %get-tuple-element.17) | copy-start | bytes 1572868

commit v6 on v5

--- a/solution.py
+++ b/solution.py
@@ -93,7 +93,7 @@
 
     @pl.loop(1, devices)
     def _(step):
-        other = (mine + 37 * step) % devices
+        other = (mine + 45 * step) % devices
         pl.semaphore_signal(
             barrier, inc=1, device_id=(other // shards, other % shards), device_id_type=pl.DeviceIdType.MESH
         )
@@ -164,7 +164,7 @@
 
         @pl.loop(max(first, 1), min(first + BATCH, devices))
         def _(step):
-            other = (mine + 37 * step) % devices
+            other = (mine + 45 * step) % devices
             pltpu.make_async_remote_copy(
                 src_ref=rows_out.at[other],
                 dst_ref=blocks_in.at[mine],
@@ -187,7 +187,7 @@
 
     batches = devices // BATCH
 
-    for batch in range(batches):
+    for batch in range(batches // 2):
         exchange_blocks(batch)
     own_copy.wait()
 
@@ -231,6 +231,9 @@
 
     load_speed = pltpu.make_async_copy(speed_ref, rows_in, side_sem.at[0])
     load_speed.start()
+
+    for batch in range(batches // 2, batches):
+        exchange_blocks(batch)
 
     third = {part: [] for part in range(len(PARTS))}
     for part, (a, b, c, begin, end) in enumerate(PARTS):
@@ -364,8 +367,11 @@
 
 
 def unspread_kernel(blocks_ref, out_ref):
-    for g in range(4):
-        out_ref[g] = blocks_ref[:, 0, g].reshape(-1, 128).T
+    shards, groups = blocks_ref.shape[1:3]
+    for i in range(shards):
+        for g in range(groups):
+            turned = blocks_ref[:, i, g].reshape(-1, 128).T
+            out_ref[g, :, i * turned.shape[1] : (i + 1) * turned.shape[1]] = turned
 
 
 def unspread(blocks, modules, rows):
@@ -373,9 +379,9 @@
     wide = paths * cols
     out = pl.pallas_call(
         unspread_kernel,
-        grid=(shards,),
-        in_specs=[pl.BlockSpec((paths, 1, groups, cols, 128), lambda i: (0, i, 0, 0, 0))],
-        out_specs=pl.BlockSpec((groups, 128, wide), lambda i: (0, 0, i)),
+        grid=(shards // 2,),
+        in_specs=[pl.BlockSpec((paths, 2, groups, cols, 128), lambda i: (0, i, 0, 0, 0))],
+        out_specs=pl.BlockSpec((groups, 128, 2 * wide), lambda i: (0, 0, i)),
         out_shape=jax.ShapeDtypeStruct((groups, 128, wide * shards), blocks.dtype),
         compiler_params=pltpu.CompilerParams(vmem_limit_bytes=VMEM_LIMIT),
         name="unspread",
@@ -578,11 +584,9 @@
         load_speed = pltpu.make_async_copy(speed_ref, speed, side_sem.at[1])
         load_speed.start()
         load_table.start()
-        loads = []
         for g in range(groups):
             part = pl.ds(4 * g, 4)
-            loads.append(pltpu.make_async_copy(sums_ref.at[part], sums.at[part], sums_sem.at[g]))
-            loads[-1].start()
+            pltpu.make_async_copy(sums_ref.at[part], sums.at[part], sums_sem.at[g]).start()
         barrier = pltpu.get_barrier_semaphore()
 
         @pl.loop(1, devices)
@@ -595,11 +599,11 @@
         swap[...] = swap_values()
         load_speed.wait()
         load_table.wait()
-        for load in loads:
-            load.wait()
 
         @pl.loop(0, groups)
         def _(group):
+            part = pl.ds(4 * group, 4)
+            pltpu.make_async_copy(sums_ref.at[part], sums.at[part], sums_sem.at[group]).wait()
             outer_step(counts_ref, sums, begun, speed, swap, updated, blocks_out, group)
 
         own_block().start()

time: 374 us -> 373 us (level)
  Pallas kernels: 358 us -> 354 us
where the time goes in v6:
time: 373 us; the launch traced here: 370 us
  Pallas kernels  354 us (95%)
  starting transfers between devices  8.99 us (2%)
  other arithmetic  3.88 us (1%)
    pallas_call x1, Pallas kernels, gather_tokens(): pl.pallas_call(gather_tokens_kernel, in_specs=[anywhere] * 4, out_specs=[...  196 us
    pallas_call x1, Pallas kernels, inner_steps(): pl.pallas_call(inner_kernel, grid_spec=pltpu.PrefetchScalarGridSpec(num_s...  79.9 us
    pallas_call x1, Pallas kernels, finish(): pl.pallas_call(finish_kernel, grid=(paths,), in_specs=[scalars, scalars,...  72.6 us
    all_to_all x1, starting transfers between devices, exchange(): return lax.all_to_all(blocks, axes, split_axis=0, concat_axis=0, tiled=True)  8.99 us
  transfers between devices with their start and end apart: 1, of which 0 were waited for; matrix products, arithmetic and copies ran while one was open for 0% of the time, Pallas kernels for 22%

profile of v6, /device:TPU:1, one launch (start us, length us, event | category | flops | bytes accessed | tf_op | source)
XLA Modules:
  0.0 370.4 jit_solution(17471293225477939252)
XLA Ops:
  0.6 1.2 fusion
  1.9 2.0 fusion.1.own_ref
  3.9 2.0 copy.12
  5.9 196.0 %gather_tokens.1 = (bf16[4,4,4,2,64,4096]{5,4,3,2,1,0:T(8,128)(2,1)}, bf16[16,32,512]{2,1,0:T(8,128)(2,1)}, bf16[16,32,4096]{2,1,0:T(8,128)(2,1)}, bf16[128,4,32,128]{3,2,1,0:T(8,128)(2,1)}) custom-call(bf16[64,4096]{1,0:T(8,128)(2,1)} %fusion.1.own_ref, bf16[16,32,512]{2,1,0:T(8,128)(2,1)} %bitcast.11, bf16[4,128,4096]{2,1,0:T(8,128)(2,1)} %bitcast.7, ...), custom_call_target="tpu_custom_call" | custom-call | bytes 134217728 | tf_op jit(solution)/shard_map/gather_tokens/pallas_call | solution.py:332
  202.0 0.0 copy-start.2
  202.0 9.0 %all-to-all-start = ((bf16[128,4,32,128]{3,2,1,0:T(8,128)(2,1)}), bf16[128,4,32,128]{3,2,1,0:T(8,128)(2,1)}, u32[]{:S(2)}, u32[]{:S(2)}) async-start(bf16[128,4,32,128]{3,2,1,0:T(8,128)(2,1)} %get-tuple-element.11), calls=%async_computation | async-start | bytes 8388608 | tf_op jit(solution)/shard_map/all_to_all | solution.py:704
  211.0 0.0 copy-done.2
  211.0 0.1 copy.11
  211.1 0.1 reshape.34.lists_ref
  211.1 0.0 copy-start.1
  211.2 0.6 convert_reduce_fusion.counts_ref
  211.8 0.0 copy-done.1
  211.8 79.9 %inner_steps.1.sums_ref = f32[16,32,4096]{2,1,0:T(8,128)} custom-call(s32[32]{0:T(128)} %copy-done.1, bf16[8192,4096]{1,0:T(8,128)(2,1)} %bitcast.4.normed_ref, bf16[16,32,512]{2,1,0:T(8,128)(2,1)} %get-tuple-element.9.goal_ref, bf16[16,32,4096]{2,1,0:T(8,128)(2,1)} %get-tuple-element.10.table_ref), custom_call_target="tpu_custom_call" | custom-call | flops 34359738368 | bytes 67108864 | tf_op jit(solution)/shard_map/inner_steps/pallas_call | solution.py:514
  291.7 0.0 all-to-all-done.speed_ref
  291.7 72.6 %finish.1 = (bf16[128,4,32,128]{3,2,1,0:T(8,128)(2,1)}, bf16[512,512]{1,0:T(8,128)(2,1)}) custom-call(s32[32]{0:T(128)} %copy-done.1, f32[16]{0:T(128)} %convert_reduce_fusion.counts_ref, bf16[8192,4096]{1,0:T(8,128)(2,1)} %bitcast.4.normed_ref, f32[16,32,4096]{2,1,0:T(8,128)} %inner_steps.1.sums_ref, bf16[16,32,4096]{2,1,0:T(8,128)(2,1)} %get-tuple-element.10.table_ref, ...), custom_call_target="tpu_custom_call" | custom-call | flops 4294967296 | bytes 67108864 | tf_op jit(solution)/shard_map/finish/pallas_call | solution.py:659
  364.3 0.0 copy-start
  364.4 5.3 %unspread.1 = bf16[4,128,4096]{2,1,0:T(8,128)(2,1)} custom-call(bf16[16,8,4,32,128]{4,3,2,1,0:T(8,128)(2,1)} %bitcast.10), custom_call_target="tpu_custom_call" | custom-call | tf_op jit(solution)/shard_map/unspread/pallas_call | solution.py:380
  369.6 0.0 copy-done
  369.6 0.8 copy.14
  (1 shorter events, 0.0 us)
Async XLA Ops:
  202.0 9.0 %copy-start.2 = (s32[16,2]{0,1:T(2,128)S(1)}, s32[16,2]{0,1:T(2,128)}, u32[]{:S(2)}) copy-start(s32[16,2]{0,1:T(2,128)} %param.9) | copy-start | bytes 388
  202.0 89.8 %all-to-all-start = ((bf16[128,4,32,128]{3,2,1,0:T(8,128)(2,1)}), bf16[128,4,32,128]{3,2,1,0:T(8,128)(2,1)}, u32[]{:S(2)}, u32[]{:S(2)}) async-start(bf16[128,4,32,128]{3,2,1,0:T(8,128)(2,1)} %get-tuple-element.11), calls=%async_computation | async-start | bytes 8388608 | tf_op jit(solution)/shard_map/all_to_all | solution.py:704
  211.1 0.6 copy-start.1
  364.3 5.3 %copy-start = (bf16[512,512]{1,0:T(8,128)(2,1)S(1)}, bf16[512,512]{1,0:T(8,128)(2,1)}, u32[]{:S(2)}) copy-start(bf16[512,512]{1,0:T(8,128)(2,1)} %get-tuple-element.17) | copy-start | bytes 1572868
